TPU v7x, 256 devices: a whole 4x4x8 slice. The times are simulated.
256 devices in a mesh: ray: 32 (over x, y, core), tile: 8 (over z).
Axes of the slice: x: 4, y: 4, z: 8, core: 2. Of those that a mesh axis runs over, the one named last changes fastest.
Arguments:
- data: float32 [262144], P(('ray', 'tile')), may hold values from -6 to 6
- blocks: bfloat16 [32, 8, 128, 128, 128], P('ray', 'tile'), may hold values from -0.1875 to 0.1875
- block_cols: int32 [32, 8, 128], P('ray', 'tile'), may hold values from 0 to 1023, as said below
- block_rows: int32 [32, 8, 128], P('ray', 'tile'), may hold values from 0 to 63
- block_counts: int32 [32, 8], P('ray', 'tile'), may hold values from 1 to 128, as said below
- reg_weight: float32 [32, 256, 128], P('tile', 'ray'), may hold values from 0.05 to 0.5
Outputs:
- model: float32 [32, 256, 128], P('tile', 'ray')
- ray_vector: float32 [262144], P(('ray', 'tile'))
Inputs may be any that keep to these rules, and one draw needn't show every extreme that they name: `block_counts`: some ray group has exactly 128 live blocks in some tile in every draw. `block_cols`: column c of a tile lies in the cells of ray index (c % 256) // 8. Of the 128 slots of one ray group in one tile, live or not, at most 8 name columns of one ray index, and in every draw 128 // 8 ray indices are named by exactly 8 slots.
All inputs are finite; a program needn't handle non-finite values.
Results may differ from a plain program's by a relative error of at most 0.0043.
Values may be sent and summed in bfloat16 or wider, within the bound.
No kernel may reach another device: no remote copies, remote signals or barrier semaphores. Data moves between devices by JAX's collectives and lax.ppermute only.
A program may use at most 64 MiB of HBM per device.

v0:
```python
import jax
import jax.numpy as jnp
from jax import lax
from jax.sharding import PartitionSpec as P

ITERS = 2


eps = 1e-06


def padded_2(cells, sides, width):
    for axis, dim in sides:
        count = lax.axis_size(axis)
        ends = count - 1
        head = lax.slice_in_dim(cells, 0, width, axis=dim)
        tail = lax.slice_in_dim(cells, cells.shape[dim] - width, cells.shape[dim], axis=dim)
        cells = jnp.concatenate(
            [
                lax.ppermute(tail, axis, [(i, (i + 1) % count) for i in range(ends)]),
                cells,
                lax.ppermute(head, axis, [((i + 1) % count, i) for i in range(ends)]),
            ],
            axis=dim,
        )
    return cells


def laplace(field):
    padded = padded_2(field, (("ray", 1), ("tile", 0)), 1)
    padded = jnp.pad(padded, ((0, 0), (0, 0), (1, 1)))
    beside = padded[2:, 1:-1, 1:-1] + padded[:-2, 1:-1, 1:-1]
    beside = beside + padded[1:-1, 2:, 1:-1] + padded[1:-1, :-2, 1:-1]
    beside = beside + padded[1:-1, 1:-1, 2:] + padded[1:-1, 1:-1, :-2]
    return 6.0 * field - beside


def shards(data, blocks, block_cols, block_rows, block_counts, reg_weight):
    values = blocks[0, 0]
    cols = block_cols[0, 0]
    rows = block_rows[0, 0]
    count = block_counts[0, 0]
    slots = values.shape[0]
    ray_width = values.shape[1]
    depth = values.shape[2]
    size_x, size_y = (reg_weight.shape[0], reg_weight.shape[1])
    ray_count = lax.axis_size("ray")
    grid_y = size_y * ray_count
    tile_cols = size_x * grid_y
    share = data.shape[0]
    group_rays = share * lax.axis_size("tile")
    row_blocks = group_rays // ray_width
    live = (jnp.arange(slots) < count)[:, None]
    raw_rays = data
    u_rays = data
    raw_cells = jnp.zeros_like(reg_weight)
    u_cells = raw_cells
    v_prev = jnp.zeros_like(reg_weight)
    alpha_prev = jnp.float32(0.0)
    for section in range(ITERS + 1):
        if section > 0:
            whole = lax.all_gather(v_prev.astype(jnp.bfloat16), "ray", axis=1, tiled=True).reshape(
                tile_cols, depth
            )
            product = jnp.einsum(
                "brc,bc->br", values, whole[cols], preferred_element_type=jnp.float32
            )
            product = jnp.where(live, product, 0.0)
            summed = jax.ops.segment_sum(product, rows, num_segments=row_blocks)
            contribution = summed.reshape(-1)
            total_rays = lax.psum_scatter(contribution, "tile", scatter_dimension=0, tiled=True)
            raw_rays = total_rays - alpha_prev * u_rays
            raw_cells = reg_weight * laplace(v_prev) - alpha_prev * u_cells
        rays_half = lax.all_gather(raw_rays.astype(jnp.bfloat16), "tile", axis=0, tiled=True)
        squares = jnp.sum(raw_rays * raw_rays) + jnp.sum(raw_cells * raw_cells)
        transpose_grouped = rays_half.reshape(row_blocks, ray_width)
        contrib = jnp.einsum(
            "brc,br->bc", values, transpose_grouped[rows], preferred_element_type=jnp.float32
        )
        partial_value = jax.ops.segment_sum(
            jnp.where(live, contrib, 0.0), cols, num_segments=tile_cols
        )
        z_field = lax.psum_scatter(
            partial_value.reshape(size_x, grid_y, depth), "ray", scatter_dimension=1, tiled=True
        ) + laplace(reg_weight * raw_cells)
        beta = jnp.sqrt(lax.psum(squares, ("ray", "tile")) + eps)
        v_raw = z_field / beta - beta * v_prev
        alpha = jnp.sqrt(lax.psum(jnp.sum(v_raw * v_raw), ("ray", "tile")) + eps)
        u_rays = raw_rays / beta
        u_cells = raw_cells / beta
        v_now = v_raw / alpha
        if section == 0:
            w_dir = v_now
            phibar = beta
            rhobar = alpha
            model = jnp.zeros_like(reg_weight)
        else:
            rho = jnp.sqrt(rhobar * rhobar + beta * beta)
            cosine = rhobar / rho
            sine = beta / rho
            theta = sine * alpha
            rhobar = -cosine * alpha
            phi = cosine * phibar
            phibar = sine * phibar
            model = model + phi / rho * w_dir
            w_dir = v_now - theta / rho * w_dir
        v_prev = v_now
        alpha_prev = alpha
    return (model, u_rays)


def solution(mesh):
    return jax.shard_map(
        shards,
        mesh=mesh,
        in_specs=(
            P(("ray", "tile")),
            P("ray", "tile", None, None, None),
            P("ray", "tile", None),
            P("ray", "tile", None),
            P("ray", "tile"),
            P("tile", "ray", None),
        ),
        out_specs=(P("tile", "ray", None), P(("ray", "tile"))),
        check_vma=False,
    )
```

profile of v0, /device:TPU:1, one launch (start us, length us, event | category | flops | bytes accessed | tf_op | source)
XLA Modules:
  0.0 626.5 jit_solution(17321096346106100567)
XLA Ops:
  7.2 1.4 fusion.72
  8.6 20.4 %all_gather.12 = bf16[8192]{0:T(1024)(128)(2,1)S(1)} all-gather(bf16[1024]{0:T(1024)(128)(2,1)S(1)} %get-tuple-element.30), channel_id=1, replica_groups=mesh['ray'=32,'tile'=8] {'tile'}, dimensions={0}, use_global_device_ids=true | all-gather | bytes 18432 | tf_op jit(solution)/shard_map/all_gather | solution.py:74
  31.1 3.4 fusion.6
  34.5 1.9 scatter_custom_fusion
  36.5 8.4 %collective-permute-start.1 = (f32[4,1,128]{2,1,0:T(1,128)S(1)}, f32[4,1,128]{2,1,0:T(1,128)S(1)}, u32[]{:S(2)}, u32[]{:S(2)}) collective-permute-start(f32[4,1,128]{2,1,0:T(1,128)S(1)} %get-tuple-element.29), channel_id=1, source_target_pairs={{8,0},{16,8},{24,16},{32,24},{40,32},{48,40},{56,48},{64,56},{72,6... | collective-permute-start | bytes 6152 | tf_op jit(solution)/shard_map/ppermute | solution.py:22
  44.8 3.1 collective-permute-start
  49.9 4.0 collective-permute-start.3
  54.0 77.0 %psum.35 = f32[]{:T(128)} all-reduce(f32[]{:T(128)} %get-tuple-element.31), channel_id=1, replica_groups=mesh['ray'=32,'tile'=8] {'ray','tile'}, use_global_device_ids=true, to_apply=%region_3.4 | all-reduce | flops 1 | bytes 8 | tf_op jit(solution)/shard_map/psum | solution.py:86
  133.1 1.4 multiply_reduce_fusion.2
  134.5 73.7 %psum.36 = f32[]{:T(128)} all-reduce(f32[]{:T(128)} %get-tuple-element.12), channel_id=1, replica_groups=mesh['ray'=32,'tile'=8] {'ray','tile'}, use_global_device_ids=true, to_apply=%region_5.6 | all-reduce | flops 1 | bytes 8 | tf_op jit(solution)/shard_map/psum | solution.py:88
  208.8 23.5 %all_gather.13 = bf16[4,256,128]{2,1,0:T(8,128)(2,1)S(1)} all-gather(bf16[4,8,128]{2,1,0:T(8,128)(2,1)S(1)} %get-tuple-element.10), channel_id=1, replica_groups=mesh['ray'=32,'tile'=8] {'ray'}, dimensions={1}, use_global_device_ids=true | all-gather | bytes 270336 | tf_op jit(solution)/shard_map/all_gather | solution.py:62
  233.1 4.4 fusion.4
  238.8 21.0 %all-reduce.4 = f32[8192]{0:T(1024)S(1)} all-reduce(f32[8192]{0:T(1024)S(1)} %bitcast.57), channel_id=3, replica_groups=mesh['ray'=32,'tile'=8] {'tile'}, use_global_device_ids=true, to_apply=%region_7.8.clone | all-reduce | flops 8192 | bytes 65536
  259.8 9.3 %collective-permute-start.5 = (f32[4,1,128]{2,1,0:T(1,128)S(1)}, f32[4,1,128]{2,1,0:T(1,128)S(1)}, u32[]{:S(2)}, u32[]{:S(2)}) collective-permute-start(f32[4,1,128]{2,1,0:T(1,128)S(1)} %get-tuple-element.27), channel_id=1, source_target_pairs={{8,0},{16,8},{24,16},{32,24},{40,32},{48,40},{56,48},{64,56},{72,6... | collective-permute-start | bytes 6152 | tf_op jit(solution)/shard_map/ppermute | solution.py:22
  269.1 2.0 collective-permute-start.4
  271.7 16.0 %all_gather.14 = bf16[8192]{0:T(1024)(128)(2,1)S(1)} all-gather(bf16[1024]{0:T(1024)(128)(2,1)S(1)} %convert_element_type.19), channel_id=1, replica_groups=mesh['ray'=32,'tile'=8] {'tile'}, dimensions={0}, use_global_device_ids=true | all-gather | bytes 18432 | tf_op jit(solution)/shard_map/all_gather | solution.py:74
  289.7 4.0 collective-permute-start.7
  293.7 3.4 fusion.2
  297.1 1.9 scatter_custom_fusion.2
  299.8 8.7 %collective-permute-start.9 = (f32[4,1,128]{2,1,0:T(1,128)S(1)}, f32[4,1,128]{2,1,0:T(1,128)S(1)}, u32[]{:S(2)}, u32[]{:S(2)}) collective-permute-start(f32[4,1,128]{2,1,0:T(1,128)S(1)} %get-tuple-element.25), channel_id=1, source_target_pairs={{8,0},{16,8},{24,16},{32,24},{40,32},{48,40},{56,48},{64,56},{72,6... | collective-permute-start | bytes 6152 | tf_op jit(solution)/shard_map/ppermute | solution.py:22
  308.5 2.0 collective-permute-start.8
  312.9 4.0 collective-permute-start.11
  318.1 76.6 %psum.37 = f32[]{:T(128)} all-reduce(f32[]{:T(128)S(6)} %add.169), channel_id=1, replica_groups=mesh['ray'=32,'tile'=8] {'ray','tile'}, use_global_device_ids=true, to_apply=%region_10.11 | all-reduce | flops 1 | bytes 8 | tf_op jit(solution)/shard_map/psum | solution.py:86
  395.8 1.4 multiply_reduce_fusion
  397.2 72.9 %psum.38 = f32[]{:T(128)} all-reduce(f32[]{:T(128)} %get-tuple-element.4), channel_id=1, replica_groups=mesh['ray'=32,'tile'=8] {'ray','tile'}, use_global_device_ids=true, to_apply=%region_14.15 | all-reduce | flops 1 | bytes 8 | tf_op jit(solution)/shard_map/psum | solution.py:88
  470.8 24.1 %all_gather.15 = bf16[4,256,128]{2,1,0:T(8,128)(2,1)S(1)} all-gather(bf16[4,8,128]{2,1,0:T(8,128)(2,1)S(1)} %get-tuple-element.2), channel_id=1, replica_groups=mesh['ray'=32,'tile'=8] {'ray'}, dimensions={1}, use_global_device_ids=true | all-gather | bytes 270336 | tf_op jit(solution)/shard_map/all_gather | solution.py:62
  495.6 4.4 fusion
  501.3 2.1 collective-permute-start.13
  503.4 3.5 collective-permute-start.12
  506.9 21.2 %all-reduce.5 = f32[8192]{0:T(1024)S(1)} all-reduce(f32[8192]{0:T(1024)S(1)} %bitcast.56), channel_id=5, replica_groups=mesh['ray'=32,'tile'=8] {'tile'}, use_global_device_ids=true, to_apply=%region_16.17.clone | all-reduce | flops 8192 | bytes 65536
  529.3 4.0 collective-permute-start.15
  536.2 81.4 %psum.39 = f32[]{:T(128)} all-reduce(f32[]{:T(128)S(6)} %add.184), channel_id=1, replica_groups=mesh['ray'=32,'tile'=8] {'ray','tile'}, use_global_device_ids=true, to_apply=%region_19.20 | all-reduce | flops 1 | bytes 8 | tf_op jit(solution)/shard_map/psum | solution.py:86
  (69 shorter events, 18.1 us)
Async XLA Ops:
  7.2 124.5 %copy-start.3 = (u32[256]{0:T(256)S(1)}, u32[256]{0:T(256)}, u32[]{:S(2)}) copy-start(u32[256]{0:T(256)} %constant.35) | copy-start | bytes 3076
  7.2 27.3 %copy-start.2 = (s32[1,1,128]{2,1,0:T(1,128)S(1)}, s32[1,1,128]{2,1,0:T(1,128)}, u32[]{:S(2)}) copy-start(s32[1,1,128]{2,1,0:T(1,128)} %param.8) | copy-start | bytes 1540
  7.2 29.2 %copy-start = (f32[4,8,128]{2,1,0:T(8,128)S(1)}, f32[4,8,128]{2,1,0:T(8,128)}, u32[]{:S(2)}) copy-start(f32[4,8,128]{2,1,0:T(8,128)} %param.11) | copy-start | bytes 49156
  7.2 125.9 %reduce-scatter.3.cloned.1.call-start = ((), (), s32[]{:S(2)}) async-start(), calls=%async_computation.2 | async-start | bytes 540672 | tf_op jit(solution)/shard_map/reduce_scatter | solution.py:83
  34.5 236.6 %copy-start.1 = (f32[1024]{0:T(1024)S(1)}, f32[1024]{0:T(1024)}, u32[]{:S(2)}) copy-start(f32[1024]{0:T(1024)} %param.6) | copy-start | bytes 12292
  36.4 359.4 %reduce-scatter.5.cloned.1.call-start = ((), (), s32[]{:S(2)}) async-start(), calls=%async_computation.3 | async-start | bytes 540672 | tf_op jit(solution)/shard_map/reduce_scatter | solution.py:83
  36.5 11.5 %collective-permute-start.1 = (f32[4,1,128]{2,1,0:T(1,128)S(1)}, f32[4,1,128]{2,1,0:T(1,128)S(1)}, u32[]{:S(2)}, u32[]{:S(2)}) collective-permute-start(f32[4,1,128]{2,1,0:T(1,128)S(1)} %get-tuple-element.29), channel_id=1, source_target_pairs={{8,0},{16,8},{24,16},{32,24},{40,32},{48,40},{56,48},{64,56},{72,6... | collective-permute-start | bytes 6152 | tf_op jit(solution)/shard_map/ppermute | solution.py:22
  44.8 3.8 collective-permute-start
  48.7 84.2 %collective-permute-start.2 = (f32[1,10,128]{2,1,0:T(8,128)S(1)}, f32[1,10,128]{2,1,0:T(8,128)S(1)}, u32[]{:S(2)}, u32[]{:S(2)}) collective-permute-start(f32[1,10,128]{2,1,0:T(8,128)S(1)} %get-tuple-element.21), channel_id=1, source_target_pairs={{1,0},{2,1},{3,2},{4,3},{5,4},{6,5},{7,6},{9,8},{10,9},{11,10},{12... | collective-permute-start | bytes 15368 | tf_op jit(solution)/shard_map/ppermute | solution.py:22
  49.9 83.0 %collective-permute-start.3 = (f32[1,10,128]{2,1,0:T(8,128)S(1)}, f32[1,10,128]{2,1,0:T(8,128)S(1)}, u32[]{:S(2)}, u32[]{:S(2)}) collective-permute-start(f32[1,10,128]{2,1,0:T(8,128)S(1)} %get-tuple-element.20), channel_id=1, source_target_pairs={{0,1},{1,2},{2,3},{3,4},{4,5},{5,6},{6,7},{8,9},{9,10},{10,11},{11... | collective-permute-start | bytes 15368 | tf_op jit(solution)/shard_map/ppermute | solution.py:20
  259.8 28.7 %collective-permute-start.5 = (f32[4,1,128]{2,1,0:T(1,128)S(1)}, f32[4,1,128]{2,1,0:T(1,128)S(1)}, u32[]{:S(2)}, u32[]{:S(2)}) collective-permute-start(f32[4,1,128]{2,1,0:T(1,128)S(1)} %get-tuple-element.27), channel_id=1, source_target_pairs={{8,0},{16,8},{24,16},{32,24},{40,32},{48,40},{56,48},{64,56},{72,6... | collective-permute-start | bytes 6152 | tf_op jit(solution)/shard_map/ppermute | solution.py:22
  269.1 19.4 %collective-permute-start.4 = (f32[4,1,128]{2,1,0:T(1,128)S(1)}, f32[4,1,128]{2,1,0:T(1,128)S(1)}, u32[]{:S(2)}, u32[]{:S(2)}) collective-permute-start(f32[4,1,128]{2,1,0:T(1,128)S(1)} %get-tuple-element.26), channel_id=1, source_target_pairs={{0,8},{8,16},{16,24},{24,32},{32,40},{40,48},{48,56},{56,64},{64,7... | collective-permute-start | bytes 6152 | tf_op jit(solution)/shard_map/ppermute | solution.py:20
  288.4 10.6 %collective-permute-start.6 = (f32[1,10,128]{2,1,0:T(8,128)S(1)}, f32[1,10,128]{2,1,0:T(8,128)S(1)}, u32[]{:S(2)}, u32[]{:S(2)}) collective-permute-start(f32[1,10,128]{2,1,0:T(8,128)S(1)} %get-tuple-element.19), channel_id=1, source_target_pairs={{1,0},{2,1},{3,2},{4,3},{5,4},{6,5},{7,6},{9,8},{10,9},{11,10},{12... | collective-permute-start | bytes 15368 | tf_op jit(solution)/shard_map/ppermute | solution.py:22
  289.7 9.3 %collective-permute-start.7 = (f32[1,10,128]{2,1,0:T(8,128)S(1)}, f32[1,10,128]{2,1,0:T(8,128)S(1)}, u32[]{:S(2)}, u32[]{:S(2)}) collective-permute-start(f32[1,10,128]{2,1,0:T(8,128)S(1)} %get-tuple-element.18), channel_id=1, source_target_pairs={{0,1},{1,2},{2,3},{3,4},{4,5},{5,6},{6,7},{8,9},{9,10},{10,11},{11... | collective-permute-start | bytes 15368 | tf_op jit(solution)/shard_map/ppermute | solution.py:20
  299.8 10.7 %collective-permute-start.9 = (f32[4,1,128]{2,1,0:T(1,128)S(1)}, f32[4,1,128]{2,1,0:T(1,128)S(1)}, u32[]{:S(2)}, u32[]{:S(2)}) collective-permute-start(f32[4,1,128]{2,1,0:T(1,128)S(1)} %get-tuple-element.25), channel_id=1, source_target_pairs={{8,0},{16,8},{24,16},{32,24},{40,32},{48,40},{56,48},{64,56},{72,6... | collective-permute-start | bytes 6152 | tf_op jit(solution)/shard_map/ppermute | solution.py:22
  308.5 3.1 collective-permute-start.8
  311.6 84.0 %collective-permute-start.10 = (f32[1,10,128]{2,1,0:T(8,128)S(1)}, f32[1,10,128]{2,1,0:T(8,128)S(1)}, u32[]{:S(2)}, u32[]{:S(2)}) collective-permute-start(f32[1,10,128]{2,1,0:T(8,128)S(1)} %get-tuple-element.17), channel_id=1, source_target_pairs={{1,0},{2,1},{3,2},{4,3},{5,4},{6,5},{7,6},{9,8},{10,9},{11,10},{12... | collective-permute-start | bytes 15368 | tf_op jit(solution)/shard_map/ppermute | solution.py:22
  312.9 82.7 %collective-permute-start.11 = (f32[1,10,128]{2,1,0:T(8,128)S(1)}, f32[1,10,128]{2,1,0:T(8,128)S(1)}, u32[]{:S(2)}, u32[]{:S(2)}) collective-permute-start(f32[1,10,128]{2,1,0:T(8,128)S(1)} %get-tuple-element.16), channel_id=1, source_target_pairs={{0,1},{1,2},{2,3},{3,4},{4,5},{5,6},{6,7},{8,9},{9,10},{10,11},{11... | collective-permute-start | bytes 15368 | tf_op jit(solution)/shard_map/ppermute | solution.py:20
  501.3 26.7 %collective-permute-start.13 = (f32[4,1,128]{2,1,0:T(1,128)S(1)}, f32[4,1,128]{2,1,0:T(1,128)S(1)}, u32[]{:S(2)}, u32[]{:S(2)}) collective-permute-start(f32[4,1,128]{2,1,0:T(1,128)S(1)} %get-tuple-element.23), channel_id=1, source_target_pairs={{8,0},{16,8},{24,16},{32,24},{40,32},{48,40},{56,48},{64,56},{72,6... | collective-permute-start | bytes 6152 | tf_op jit(solution)/shard_map/ppermute | solution.py:22
  503.4 24.7 %collective-permute-start.12 = (f32[4,1,128]{2,1,0:T(1,128)S(1)}, f32[4,1,128]{2,1,0:T(1,128)S(1)}, u32[]{:S(2)}, u32[]{:S(2)}) collective-permute-start(f32[4,1,128]{2,1,0:T(1,128)S(1)} %get-tuple-element.22), channel_id=1, source_target_pairs={{0,8},{8,16},{16,24},{24,32},{32,40},{40,48},{48,56},{56,64},{64,7... | collective-permute-start | bytes 6152 | tf_op jit(solution)/shard_map/ppermute | solution.py:20
  528.0 6.0 collective-permute-start.14
  529.3 4.8 collective-permute-start.15
Sparse Core Ops, SparseCore 0:
  36.5 86.9 reduce-scatter.2
  299.1 84.2 reduce-scatter.4
where the time goes:
time: 628 us; the launch traced here: 626 us
  blocking collectives  508 us (81%)
  starting transfers between devices  60.2 us (10%)
  between operations  22.2 us (4%)
  matrix products  15.6 us (2%)
  other arithmetic  15.4 us (2%)
    psum x3, blocking collectives, shards(): beta = jnp.sqrt(lax.psum(squares, ('ray', 'tile')) + eps)  235 us
    psum x2, blocking collectives, shards(): alpha = jnp.sqrt(lax.psum(jnp.sum(v_raw * v_raw), ('ray', 'tile')) + eps)  147 us
    all_gather x2, blocking collectives, shards(): lax.all_gather(v_prev.astype(jnp.bfloat16), 'ray', axis=1, tiled=True)  47.6 us
    unnamed x2, blocking collectives  42.1 us
    all_gather x2, blocking collectives, shards(): lax.all_gather(raw_rays.astype(jnp.bfloat16), 'tile', axis=0, tiled=True)  36.4 us
    ppermute x8, starting transfers between devices, padded_2(): lax.ppermute(head, axis, [((i + 1) % count, i) for i in range(ends)])  33.5 us
    ppermute x8, starting transfers between devices, padded_2(): lax.ppermute(tail, axis, [(i, (i + 1) % count) for i in range(ends)])  26.6 us
  transfers between devices with their start and end apart: 18, of which 3 were waited for; matrix products, arithmetic and copies ran while one was open for 1% of the time, Pallas kernels for 0%

commit v1 on v0

v1 whole, which is shorter than its diff:
```python
import jax
import jax.numpy as jnp
from jax import lax
from jax.experimental import pallas as pl
from jax.experimental.pallas import tpu as pltpu
from jax.sharding import PartitionSpec as P

RAY = 32
TILE = 8
CAP = 8
CX = 4
CY = 8
CELLS = CX * CY
SLOTS = 128
LANES = 128
KB = 64
KOWN = KB // TILE
MSG = 2 * CAP
TMSG = KB + CELLS + 16
eps = 1e-06

F32 = jnp.float32
BF16 = jnp.bfloat16


def iota(shape, dim):
    return lax.broadcasted_iota(jnp.int32, shape, dim)


def dot(a, b, ca, cb):
    return lax.dot_general(a, b, (((ca,), (cb,)), ((), ())), preferred_element_type=F32)


def onehot_dot(hot, x, ca, cb):
    high = x.astype(BF16)
    rest = x - high.astype(F32)
    mid = rest.astype(BF16)
    low = (rest - mid.astype(F32)).astype(BF16)
    return dot(hot, high, ca, cb) + (dot(hot, mid, ca, cb) + dot(hot, low, ca, cb))


def total(x):
    return jnp.sum(jnp.sum(x, axis=0, keepdims=True), axis=1, keepdims=True)


def wide(x):
    return jnp.broadcast_to(x, (1, LANES))


def lane_sides(f):
    lane = iota(f.shape, 1)
    left = jnp.where(lane == 0, 0.0, pltpu.roll(f, 1, 1))
    right = jnp.where(lane == LANES - 1, 0.0, pltpu.roll(f, LANES - 1, 1))
    return left + right


def row_sides(f, low, high):
    row = iota(f.shape, 0)
    below = jnp.where(row == 0, low, pltpu.roll(f, 1, 0))
    above = jnp.where(row == CY - 1, high, pltpu.roll(f, CY - 1, 0))
    return below + above


def products_t(rays, blocks, r_hot):
    picked = dot(r_hot, rays.astype(BF16), 0, 0)
    row = iota((8, LANES), 0)
    out = []
    for q in range(SLOTS // 8):
        p = picked[8 * q : 8 * q + 8, :]
        lhs = jnp.concatenate([jnp.where(row == i, p, 0.0) for i in range(8)], axis=1)
        out.append(dot(lhs.astype(BF16), blocks[8 * q : 8 * q + 8].reshape(8 * LANES, LANES), 1, 0))
    return jnp.concatenate(out, axis=0)


def products(x_t, blocks, r_hot):
    lane = iota((LANES, SLOTS), 1)
    half = SLOTS // 2
    rhs = jnp.concatenate(
        [jnp.where(lane < half, x_t, 0.0), jnp.where(lane >= half, x_t, 0.0)], axis=0
    ).astype(BF16)
    acc = jnp.zeros((LANES, SLOTS), F32)
    for b in range(half):
        res = dot(jnp.concatenate([blocks[b], blocks[b + half]], axis=1), rhs, 1, 0)
        acc = jnp.where((lane == b) | (lane == b + half), res, acc)
    return onehot_dot(r_hot, acc, 1, 1)


def send_edges(send, tile8, scratch, rows_low, rows_high, scalar, ray):
    for x in range(CX):
        scratch[0, x : x + 1, :] = rows_low[x]
        scratch[1, x : x + 1, :] = rows_high[x]
    filler = jnp.broadcast_to(scalar, (8 - CX, LANES))
    scratch[0, CX:8, :] = filler
    scratch[1, CX:8, :] = filler
    low, high = scratch[0], scratch[1]
    for d in range(RAY):
        send[d, CAP:MSG, :] = jnp.where(d > ray, high, low)


def kernel_start(pos_ref, recv, cols, rows, count, blocks, send, p_out, r_out):
    col = cols[...]
    live = iota((1, SLOTS), 1) < count[0, 0]
    slab = RAY * CY
    owner = lax.div(lax.rem(col, slab), CY)
    local = lax.div(col, slab) * CY + lax.rem(col, CY)
    own_hot = iota((RAY, SLOTS), 0) == owner
    before = (iota((SLOTS, SLOTS), 0) < iota((SLOTS, SLOTS), 1)).astype(F32).astype(BF16)
    earlier = dot(own_hot.astype(F32).astype(BF16), before, 1, 0)
    rank = jnp.sum(jnp.where(own_hot, earlier, 0.0), axis=0, keepdims=True).astype(jnp.int32)
    p_bool = (iota((RAY * CAP, SLOTS), 0) == owner * CAP + rank) & live
    p_f = p_bool.astype(F32)
    p_hot = p_f.astype(BF16)
    r_hot = ((iota((KB, SLOTS), 0) == rows[...]) & live).astype(F32).astype(BF16)
    p_out[...] = p_hot
    r_out[...] = r_hot
    data = recv[:, 0:KOWN, :].reshape(KB, LANES)
    contrib = products_t(data, blocks, r_hot)
    send[:, 0:CAP, :] = onehot_dot(p_hot, contrib, 1, 0).reshape(RAY, CAP, LANES)
    ids = jnp.sum(p_f * (local + 1).astype(F32), axis=1, keepdims=True) - 1.0
    lane = iota((RAY * CAP, LANES), 1)
    note = jnp.where(lane < LANES // 2, ids, total(data * data))
    send[:, CAP:MSG, :] = note.reshape(RAY, CAP, LANES)


def spread(send, q_hot, v_raw):
    send[:, 0:CAP, :] = onehot_dot(q_hot, v_raw, 1, 0).reshape(RAY, CAP, LANES)


def kernel_first_v(pos_ref, recv, send, v_out, q_out, beta_out, scratch):
    contrib = recv[:, 0:CAP, :].reshape(RAY * CAP, LANES)
    note = recv[:, CAP:MSG, :].reshape(RAY * CAP, LANES)
    lane = iota((RAY * CAP, LANES), 1)
    row = iota((RAY * CAP, LANES), 0)
    q_hot = ((note == lane.astype(F32)) & (lane < CELLS)).astype(F32).astype(BF16)
    q_out[...] = q_hot
    squares = total(jnp.where((lane == LANES - 1) & (lax.rem(row, CAP) == 0), note, 0.0))
    beta = jnp.sqrt(squares + eps)
    beta_out[...] = wide(beta)
    v_raw = onehot_dot(q_hot, contrib, 0, 0) / beta
    v_out[...] = v_raw[0:CELLS]
    spread(send, q_hot, v_raw)
    low = [v_raw[CY * x : CY * x + 1, :] for x in range(CX)]
    high = [v_raw[CY * x + CY - 1 : CY * x + CY, :] for x in range(CX)]
    send_edges(send, None, scratch, low, high, total(v_raw * v_raw), pos_ref[0])


def kernel_forward(pos_ref, recv, p_hot, r_hot, blocks, v_raw, send):
    ray = pos_ref[0]
    values = recv[:, 0:CAP, :].reshape(RAY * CAP, LANES).astype(BF16)
    x_t = dot(values, p_hot[...], 0, 0)
    part = products(x_t, blocks, r_hot[...])
    norm = jnp.zeros((8, LANES), F32)
    for d in range(RAY):
        norm = norm + recv[d, CAP:MSG, :]
    row = iota((8, LANES), 0)
    low = jnp.where(ray > 0, recv[jnp.maximum(ray - 1, 0), CAP:MSG, :], 0.0)
    high = jnp.where(ray < RAY - 1, recv[jnp.minimum(ray + 1, RAY - 1), CAP:MSG, :], 0.0)
    low = jnp.where(row < CX, low, norm)
    high = jnp.where(row < CX, high, norm)
    mine = v_raw[...]
    for t in range(TILE):
        send[t, 0:KB, :] = part
        send[t, KB : KB + CELLS, :] = mine
        send[t, KB + CELLS : KB + CELLS + 8, :] = low
        send[t, KB + CELLS + 8 : TMSG, :] = high


def gathered(recv):
    kv = recv[0, 0:KB, :]
    norm = recv[0, TMSG - 1 : TMSG, :]
    for t in range(1, TILE):
        kv = kv + recv[t, 0:KB, :]
        norm = norm + recv[t, TMSG - 1 : TMSG, :]
    return kv, jnp.sqrt(norm + eps)


def slab_laplace(recv, index):
    t, x = divmod(index, CX)

    def cells(i):
        t, x = divmod(i, CX)
        start = KB + CY * x
        return recv[t, start : start + CY, :]

    f = cells(index)
    base = KB + CELLS + x
    beside = row_sides(f, recv[t, base : base + 1, :], recv[t, base + 8 : base + 9, :])
    beside = beside + lane_sides(f)
    if index > 0:
        beside = beside + cells(index - 1)
    if index < TILE * CX - 1:
        beside = beside + cells(index + 1)
    return 6.0 * f - beside


def kernel_back(
    pos_ref, recv, start, beta0, blocks, p_hot, r_hot, send, raw1_out, raw2_out, alpha_out, nq_out, scratch, field
):
    ray, tile = pos_ref[0], pos_ref[1]
    kv, alpha = gathered(recv)
    alpha_out[...] = alpha
    data = start[:, 0:KOWN, :].reshape(KB, LANES)
    raw1 = kv / alpha - alpha * (data / beta0[...])
    raw1_out[...] = raw1
    field[0] = jnp.zeros((CY, LANES), F32)
    field[TILE * CX + 1] = jnp.zeros((CY, LANES), F32)
    squares = jnp.zeros((CY, LANES), F32)
    for i in range(TILE * CX):
        t, x = divmod(i, CX)
        weight = start[t, KOWN + CY * x : KOWN + CY * x + CY, :]
        raw2 = weight * (slab_laplace(recv, i) / alpha)
        raw2_out[i] = raw2
        squares = squares + raw2 * raw2
        field[i + 1] = weight * raw2
    contrib = products_t(raw1, blocks, r_hot[...])
    send[:, 0:CAP, :] = onehot_dot(p_hot[...], contrib, 1, 0).reshape(RAY, CAP, LANES)
    low, high = [], []
    for x in range(CX):
        at = tile * CX + x + 1
        f = field[at]
        beside = row_sides(f, 0.0, 0.0) + lane_sides(f) + field[at - 1] + field[at + 1]
        nq_out[CY * x : CY * x + CY, :] = 6.0 * f - beside
        low.append(f[0:1])
        high.append(f[CY - 1 : CY])
    send_edges(send, None, scratch, low, high, total(raw1 * raw1) + total(squares), ray)


def kernel_next_v(pos_ref, recv, q_ref, v0_raw, alpha0, nq, send, v_out, beta_out, scratch):
    ray = pos_ref[0]
    contrib = recv[:, 0:CAP, :].reshape(RAY * CAP, LANES)
    q_hot = q_ref[...]
    norm = recv[0, MSG - 1 : MSG, :]
    for d in range(1, RAY):
        norm = norm + recv[d, MSG - 1 : MSG, :]
    beta = jnp.sqrt(norm + eps)
    beta_out[...] = beta
    z = onehot_dot(q_hot, contrib, 0, 0)
    low = jnp.where(ray > 0, recv[jnp.maximum(ray - 1, 0), CAP:MSG, :], 0.0)
    high = jnp.where(ray < RAY - 1, recv[jnp.minimum(ray + 1, RAY - 1), CAP:MSG, :], 0.0)
    row = iota((CY, LANES), 0)
    squares = jnp.zeros((CY, LANES), F32)
    edges_low, edges_high, parts = [], [], []
    for x in range(CX):
        cut = slice(CY * x, CY * x + CY)
        edge = jnp.where(row == 0, low[x : x + 1], 0.0) + jnp.where(row == CY - 1, high[x : x + 1], 0.0)
        v_raw = (z[cut] + (nq[cut, :] - edge)) / beta - beta * (v0_raw[cut, :] / alpha0[...])
        parts.append(v_raw)
        squares = squares + v_raw * v_raw
        edges_low.append(v_raw[0:1])
        edges_high.append(v_raw[CY - 1 : CY])
    v_raw = jnp.concatenate(parts, axis=0)
    v_out[...] = v_raw
    spread(send, q_hot, jnp.concatenate([v_raw, jnp.zeros((LANES - CELLS, LANES), F32)], axis=0))
    send_edges(send, None, scratch, edges_low, edges_high, total(squares), ray)


def kernel_last_norm(pos_ref, recv, start, beta1, raw1_ref, raw2_ref, send, raw1_out, alpha_out, scratch):
    tile = pos_ref[1]
    kv, alpha = gathered(recv)
    alpha_out[...] = alpha
    raw1 = kv / alpha - alpha * (raw1_ref[...] / beta1[...])
    scratch[...] = raw1.reshape(TILE, KOWN, LANES)
    raw1_out[...] = scratch[tile]
    squares = jnp.zeros((CY, LANES), F32)
    for i in range(TILE * CX):
        t, x = divmod(i, CX)
        weight = start[t, KOWN + CY * x : KOWN + CY * x + CY, :]
        raw2 = weight * (slab_laplace(recv, i) / alpha) - alpha * (raw2_ref[i] / beta1[...])
        squares = squares + raw2 * raw2
    norm = total(raw1 * raw1) + total(squares)
    send[...] = jnp.broadcast_to(norm.reshape(1, 1, 1), (RAY, 1, LANES))


def kernel_end(recv, v0_raw, v1_raw, raw1, beta0, beta1, alpha0, alpha1, model_out, u_out):
    norm = recv[0]
    for d in range(1, RAY):
        norm = norm + recv[d]
    b0, b1, b2 = beta0[...], beta1[...], jnp.sqrt(norm + eps)
    a0, a1 = alpha0[...], alpha1[...]
    v0, v1 = v0_raw[...] / a0, v1_raw[...] / a1
    rho1 = jnp.sqrt(a0 * a0 + b1 * b1)
    cosine1, sine1 = a0 / rho1, b1 / rho1
    theta = sine1 * a1
    rhobar = -cosine1 * a1
    phi1, phibar = cosine1 * b0, sine1 * b0
    w1 = v1 - theta / rho1 * v0
    rho2 = jnp.sqrt(rhobar * rhobar + b2 * b2)
    phi2 = rhobar / rho2 * phibar
    model_out[...] = phi1 / rho1 * v0 + phi2 / rho2 * w1
    u_out[...] = raw1[...] / b2


VM = pl.BlockSpec(memory_space=pltpu.VMEM)
SM = pl.BlockSpec(memory_space=pltpu.SMEM)


def call(kernel, outs, args, specs=None, scratch=()):
    return pl.pallas_call(
        kernel,
        out_shape=[jax.ShapeDtypeStruct(shape, kind) for shape, kind in outs],
        in_specs=specs or [VM] * len(args),
        out_specs=[VM] * len(outs),
        scratch_shapes=[pltpu.VMEM(shape, F32) for shape in scratch],
        compiler_params=pltpu.CompilerParams(vmem_limit_bytes=32 * 2**20),
        name=kernel.__name__,
    )(*args)


def shards(data, blocks, block_cols, block_rows, block_counts, reg_weight):
    pos = jnp.stack([lax.axis_index("ray"), lax.axis_index("tile")]).astype(jnp.int32)
    values = blocks[0, 0]
    own = jnp.concatenate([data.reshape(KOWN, LANES), reg_weight.reshape(CELLS, LANES)], axis=0)
    start = lax.all_to_all(jnp.broadcast_to(own, (TILE,) + own.shape), "tile", 0, 0)
    message = ((RAY, MSG, LANES), F32)
    tile_message = ((TILE, TMSG, LANES), F32)
    scalar = ((1, LANES), F32)
    cells = ((CELLS, LANES), F32)
    edges = (2, 8, LANES)
    send, p_hot, r_hot = call(
        kernel_start,
        [message, ((RAY * CAP, SLOTS), BF16), ((KB, SLOTS), BF16)],
        (pos, start, block_cols[0], block_rows[0], block_counts, values),
        [SM, VM, VM, VM, SM, VM],
    )
    recv = lax.all_to_all(send, "ray", 0, 0)
    send, v0_raw, q_hot, beta0 = call(
        kernel_first_v,
        [message, cells, ((RAY * CAP, LANES), BF16), scalar],
        (pos, recv),
        [SM, VM],
        [edges],
    )
    recv = lax.all_to_all(send, "ray", 0, 0)
    (send,) = call(
        kernel_forward, [tile_message], (pos, recv, p_hot, r_hot, values, v0_raw), [SM] + [VM] * 5
    )
    recv = lax.all_to_all(send, "tile", 0, 0)
    send, raw1, raw2, alpha0, nq = call(
        kernel_back,
        [message, ((KB, LANES), F32), ((TILE * CX, CY, LANES), F32), scalar, cells],
        (pos, recv, start, beta0, values, p_hot, r_hot),
        [SM] + [VM] * 6,
        [edges, (TILE * CX + 2, CY, LANES)],
    )
    recv = lax.all_to_all(send, "ray", 0, 0)
    send, v1_raw, beta1 = call(
        kernel_next_v,
        [message, cells, scalar],
        (pos, recv, q_hot, v0_raw, alpha0, nq),
        [SM] + [VM] * 5,
        [edges],
    )
    recv = lax.all_to_all(send, "ray", 0, 0)
    (send,) = call(
        kernel_forward, [tile_message], (pos, recv, p_hot, r_hot, values, v1_raw), [SM] + [VM] * 5
    )
    recv = lax.all_to_all(send, "tile", 0, 0)
    send, raw1_own, alpha1 = call(
        kernel_last_norm,
        [((RAY, 1, LANES), F32), ((KOWN, LANES), F32), scalar],
        (pos, recv, start, beta1, raw1, raw2),
        [SM] + [VM] * 5,
        [(TILE, KOWN, LANES)],
    )
    recv = lax.all_to_all(send, "ray", 0, 0)
    model, rays = call(
        kernel_end,
        [cells, ((KOWN, LANES), F32)],
        (recv, v0_raw, v1_raw, raw1_own, beta0, beta1, alpha0, alpha1),
    )
    return model.reshape(reg_weight.shape), rays.reshape(data.shape)


def solution(mesh):
    return jax.shard_map(
        shards,
        mesh=mesh,
        in_specs=(
            P(("ray", "tile")),
            P("ray", "tile", None, None, None),
            P("ray", "tile", None),
            P("ray", "tile", None),
            P("ray", "tile"),
            P("tile", "ray", None),
        ),
        out_specs=(P("tile", "ray", None), P(("ray", "tile"))),
        check_vma=False,
    )
```

time: 628 us -> 139 us (0.22)
  blocking collectives: 508 us -> 104 us
  starting transfers between devices: 60.2 us -> 9.01 us
  between operations: 22.2 us -> 1.35 us
  matrix products: 15.6 us -> 0 us
  other arithmetic: 15.4 us -> 0.8 us
  Pallas kernels: 0 us -> 10.9 us
    psum x5 -> x0, blocking collectives: 382 us -> none  [the longest x3 235 us: shards(): beta = jnp.sqrt(lax.psum(squares, ('ray', 'tile')) + eps)]
    all_to_all x0 -> x7, blocking collectives: none -> 104 us  [the longest x5 66.4 us: shards(): recv = lax.all_to_all(send, 'ray', 0, 0)]
    all_gather x4 -> x0, blocking collectives: 84 us -> none  [the longest x2 47.6 us: shards(): lax.all_gather(v_prev.astype(jnp.bfloat16), 'ray', axis=1, tiled=True)]
    ppermute x16 -> x0, starting transfers between devices: 60.1 us -> none  [the longest x8 33.5 us: padded_2(): lax.ppermute(head, axis, [((i + 1) % count, i) for i in range(ends)])]
    unnamed x2 -> x0, blocking collectives: 42.1 us -> none
    dot_general x4 -> x0, matrix products: 15.6 us -> none  [the longest x2 8.86 us: shards(): jnp.einsum('brc,bc->br', values, whole[cols], preferred_element_type=jnp....]
    pallas_call x0 -> x8, Pallas kernels: none -> 10.9 us  [call(): pl.pallas_call(kernel, out_shape=[jax.ShapeDtypeStruct(shape, kind) for s...]
    all_to_all x0 -> x1, starting transfers between devices: none -> 9.01 us  [shards(): lax.all_to_all(jnp.broadcast_to(own, (TILE,) + own.shape), 'tile', 0, 0)]
  transfers between devices with their start and end apart: 18 -> 1, of which waited for: 3 -> 1; matrix products, arithmetic and copies ran while one was open for 1% -> 0% of each run, Pallas kernels for 0% -> 0%
where the time goes in v1:
time: 139 us; the launch traced here: 138 us
  blocking collectives  104 us (75%)
  Pallas kernels  10.9 us (8%)
  starting transfers between devices  9.01 us (6%)
  waiting for transfers between devices  7.42 us (5%)
  local copies, waits for them, and re-layouts  4.17 us (3%)
    all_to_all x5, blocking collectives, shards(): recv = lax.all_to_all(send, 'ray', 0, 0)  66.4 us
    all_to_all x2, blocking collectives, shards(): recv = lax.all_to_all(send, 'tile', 0, 0)  38 us
    pallas_call x8, Pallas kernels, call(): pl.pallas_call(kernel, out_shape=[jax.ShapeDtypeStruct(shape, kind) for s...  10.9 us
    all_to_all x1, starting transfers between devices, shards(): lax.all_to_all(jnp.broadcast_to(own, (TILE,) + own.shape), 'tile', 0, 0)  9.01 us
    all_to_all x1, waiting for transfers between devices, shards(): lax.all_to_all(jnp.broadcast_to(own, (TILE,) + own.shape), 'tile', 0, 0)  7.42 us
    unnamed x8, local copies, waits for them, and re-layouts  3.5 us
  transfers between devices with their start and end apart: 1, of which 1 were waited for; matrix products, arithmetic and copies ran while one was open for 0% of the time, Pallas kernels for 0%

profile of v1, /device:TPU:1, one launch (start us, length us, event | category | flops | bytes accessed | tf_op | source)
XLA Modules:
  0.0 138.0 jit_solution(6311373264209762143)
XLA Ops:
  0.6 0.7 pad_maximum_fusion
  1.4 0.7 broadcast_in_dim.3
  2.0 9.0 %all-to-all-start = ((f32[8,40,128]{2,1,0:T(8,128)}), f32[8,40,128]{2,1,0:T(8,128)S(1)}, u32[]{:S(2)}, u32[]{:S(2)}) async-start(f32[8,40,128]{2,1,0:T(8,128)} %broadcast_in_dim.3), calls=%async_computation | async-start | bytes 327680 | tf_op jit(solution)/shard_map/all_to_all | solution.py:313
  11.7 0.1 pad_add_fusion.pos_ref
  11.8 7.4 %all-to-all-done.recv.start = f32[8,40,128]{2,1,0:T(8,128)S(1)} async-done(((f32[8,40,128]{2,1,0:T(8,128)}), f32[8,40,128]{2,1,0:T(8,128)S(1)}, u32[]{:S(2)}, u32[]{:S(2)}) %all-to-all-start) | async-done | bytes 163872 | tf_op jit(solution)/shard_map/all_to_all | solution.py:313
  19.2 0.0 copy-start
  19.2 2.2 %copy-done = bf16[1,1,128,128,128]{4,3,2,1,0:T(8,128)(2,1)S(1)} copy-done((bf16[1,1,128,128,128]{4,3,2,1,0:T(8,128)(2,1)S(1)}, bf16[1,1,128,128,128]{4,3,2,1,0:T(8,128)(2,1)}, u32[]{:S(2)}) %copy-start) | copy-done | bytes 4194328
  21.4 0.0 copy-start.2
  21.4 0.7 copy-done.2
  22.0 0.0 copy-start.3
  22.0 0.7 copy-done.3
  22.7 0.0 copy-start.1
  22.7 1.6 %kernel_start.1 = (f32[32,16,128]{2,1,0:T(8,128)S(1)}, bf16[256,128]{1,0:T(8,128)(2,1)S(1)}, bf16[64,128]{1,0:T(8,128)(2,1)S(1)}) custom-call(s32[2]{0:T(128)S(1)} %pad_add_fusion.pos_ref, f32[8,40,128]{2,1,0:T(8,128)S(1)} %all-to-all-done.recv.start, s32[1,128]{1,0:T(1,128)S(1)} %bitcast.13, s32[1,128]{1,0:T(1,128)S(1)} %bitcast.14, s32[1,1]{1,0:T(1,128)S(6)} %copy.8.count, ...), custom_call_target="tpu_custom_call" | custom-call | tf_op jit(solution)/shard_map/kernel_start/pallas_call | solution.py:298
  24.3 18.4 %all_to_all.40.recv = f32[32,16,128]{2,1,0:T(8,128)S(1)} all-to-all(f32[32,16,128]{2,1,0:T(8,128)S(1)} %get-tuple-element.22), channel_id=1, replica_groups=mesh['ray'=32,'tile'=8] {'ray'}, dimensions={0} | all-to-all | bytes 524288 | tf_op jit(solution)/shard_map/all_to_all | solution.py:325
  42.7 1.1 kernel_first_v.1
  43.8 12.5 %all_to_all.41.recv = f32[32,16,128]{2,1,0:T(8,128)S(1)} all-to-all(f32[32,16,128]{2,1,0:T(8,128)S(1)} %get-tuple-element.23), channel_id=1, replica_groups=mesh['ray'=32,'tile'=8] {'ray'}, dimensions={0} | all-to-all | bytes 524288 | tf_op jit(solution)/shard_map/all_to_all | solution.py:333
  56.2 0.0 copy-done.1
  56.2 2.1 %kernel_forward.2 = f32[8,112,128]{2,1,0:T(8,128)S(1)} custom-call(s32[2]{0:T(128)S(1)} %pad_add_fusion.pos_ref, f32[32,16,128]{2,1,0:T(8,128)S(1)} %all_to_all.41.recv, bf16[256,128]{1,0:T(8,128)(2,1)S(1)} %get-tuple-element.24.p_hot, bf16[64,128]{1,0:T(8,128)(2,1)S(1)} %get-tuple-element.25.r_hot, bf16[128,128,128]{2,1,0:T(8,128)(2,1)S(1)} %bitcast.10, ...), custom_call_target="tpu_custom_call" | custom-call | tf_op jit(solution)/shard_map/kernel_forward/pallas_call | solution.py:298
  58.4 19.0 %all_to_all.42.recv = f32[8,112,128]{2,1,0:T(8,128)S(1)} all-to-all(f32[8,112,128]{2,1,0:T(8,128)S(1)} %kernel_forward.2), channel_id=1, replica_groups=mesh['ray'=32,'tile'=8] {'tile'}, dimensions={0} | all-to-all | bytes 917504 | tf_op jit(solution)/shard_map/all_to_all | solution.py:337
  77.4 1.6 %kernel_back.1 = (f32[32,16,128]{2,1,0:T(8,128)S(1)}, f32[64,128]{1,0:T(8,128)S(1)}, f32[32,8,128]{2,1,0:T(8,128)S(1)}, f32[1,128]{1,0:T(1,128)S(1)}, f32[32,128]{1,0:T(8,128)S(1)}) custom-call(s32[2]{0:T(128)S(1)} %pad_add_fusion.pos_ref, f32[8,112,128]{2,1,0:T(8,128)S(1)} %all_to_all.42.recv, f32[8,40,128]{2,1,0:T(8,128)S(1)} %all-to-all-done.recv.start, ...), custom_call_target="tpu_custom_call" | custom-call | tf_op jit(solution)/shard_map/kernel_back/pallas_call | solution.py:298
  78.9 12.5 %all_to_all.43.recv = f32[32,16,128]{2,1,0:T(8,128)S(1)} all-to-all(f32[32,16,128]{2,1,0:T(8,128)S(1)} %get-tuple-element.28), channel_id=1, replica_groups=mesh['ray'=32,'tile'=8] {'ray'}, dimensions={0} | all-to-all | bytes 524288 | tf_op jit(solution)/shard_map/all_to_all | solution.py:345
  91.5 1.0 kernel_next_v.1
  92.5 12.5 %all_to_all.44.recv = f32[32,16,128]{2,1,0:T(8,128)S(1)} all-to-all(f32[32,16,128]{2,1,0:T(8,128)S(1)} %get-tuple-element.32), channel_id=1, replica_groups=mesh['ray'=32,'tile'=8] {'ray'}, dimensions={0} | all-to-all | bytes 524288 | tf_op jit(solution)/shard_map/all_to_all | solution.py:353
  104.9 2.1 %kernel_forward.3 = f32[8,112,128]{2,1,0:T(8,128)S(1)} custom-call(s32[2]{0:T(128)S(1)} %pad_add_fusion.pos_ref, f32[32,16,128]{2,1,0:T(8,128)S(1)} %all_to_all.44.recv, bf16[256,128]{1,0:T(8,128)(2,1)S(1)} %get-tuple-element.24.p_hot, bf16[64,128]{1,0:T(8,128)(2,1)S(1)} %get-tuple-element.25.r_hot, bf16[128,128,128]{2,1,0:T(8,128)(2,1)S(1)} %bitcast.12, ...), custom_call_target="tpu_custom_call" | custom-call | tf_op jit(solution)/shard_map/kernel_forward/pallas_call | solution.py:298
  107.1 19.0 %all_to_all.45.recv = f32[8,112,128]{2,1,0:T(8,128)S(1)} all-to-all(f32[8,112,128]{2,1,0:T(8,128)S(1)} %kernel_forward.3), channel_id=1, replica_groups=mesh['ray'=32,'tile'=8] {'tile'}, dimensions={0} | all-to-all | bytes 917504 | tf_op jit(solution)/shard_map/all_to_all | solution.py:357
  126.1 0.8 kernel_last_norm.1
  126.9 10.5 %all_to_all.46.recv = f32[32,1,128]{2,1,0:T(1,128)S(1)} all-to-all(f32[32,1,128]{2,1,0:T(1,128)S(1)} %get-tuple-element.37), channel_id=1, replica_groups=mesh['ray'=32,'tile'=8] {'ray'}, dimensions={0} | all-to-all | bytes 32768 | tf_op jit(solution)/shard_map/all_to_all | solution.py:365
  137.3 0.7 kernel_end.1
Async XLA Ops:
  2.0 17.2 %all-to-all-start = ((f32[8,40,128]{2,1,0:T(8,128)}), f32[8,40,128]{2,1,0:T(8,128)S(1)}, u32[]{:S(2)}, u32[]{:S(2)}) async-start(f32[8,40,128]{2,1,0:T(8,128)} %broadcast_in_dim.3), calls=%async_computation | async-start | bytes 327680 | tf_op jit(solution)/shard_map/all_to_all | solution.py:313
  19.2 2.2 %copy-start = (bf16[1,1,128,128,128]{4,3,2,1,0:T(8,128)(2,1)S(1)}, bf16[1,1,128,128,128]{4,3,2,1,0:T(8,128)(2,1)}, u32[]{:S(2)}) copy-start(bf16[1,1,128,128,128]{4,3,2,1,0:T(8,128)(2,1)} %param.7) | copy-start | bytes 12582916
  21.4 0.7 copy-start.2
  22.0 0.7 copy-start.3
  22.7 33.5 %copy-start.1 = (bf16[1,1,128,128,128]{4,3,2,1,0:T(8,128)(2,1)S(1)}, bf16[1,1,128,128,128]{4,3,2,1,0:T(8,128)(2,1)}, u32[]{:S(2)}) copy-start(bf16[1,1,128,128,128]{4,3,2,1,0:T(8,128)(2,1)} %param.7) | copy-start | bytes 12582916

commit v2 on v1

v2 whole, which is shorter than its diff:
```python
import jax
import jax.numpy as jnp
from jax import lax
from jax.experimental import pallas as pl
from jax.experimental.pallas import tpu as pltpu
from jax.sharding import PartitionSpec as P

RAY = 32
TILE = 8
CAP = 8
CX = 4
CY = 8
CELLS = CX * CY
SLOTS = 128
LANES = 128
KB = 64
KOWN = KB // TILE
MSG = 2 * CAP
TMSG = KB + CELLS + 16
SMSG = KOWN + CELLS
XS = TILE * CX
eps = 1e-06

F32 = jnp.float32
BF16 = jnp.bfloat16


def iota(shape, dim):
    return lax.broadcasted_iota(jnp.int32, shape, dim)


def dot(a, b, ca, cb):
    return lax.dot_general(a, b, (((ca,), (cb,)), ((), ())), preferred_element_type=F32)


def onehot_dot(hot, x, ca, cb):
    high = x.astype(BF16)
    rest = x - high.astype(F32)
    mid = rest.astype(BF16)
    low = (rest - mid.astype(F32)).astype(BF16)
    return dot(hot, high, ca, cb) + (dot(hot, mid, ca, cb) + dot(hot, low, ca, cb))


def total(x):
    return jnp.sum(jnp.sum(x, axis=0, keepdims=True), axis=1, keepdims=True)


def terms(x):
    high = x.astype(BF16).astype(F32)
    mid = (x - high).astype(BF16).astype(F32)
    return high, mid, x - high - mid


def wide(x):
    return jnp.broadcast_to(x, (1, LANES))


def lane_sides(f):
    lane = iota(f.shape, 1)
    left = jnp.where(lane == 0, 0.0, pltpu.roll(f, 1, 1))
    right = jnp.where(lane == LANES - 1, 0.0, pltpu.roll(f, LANES - 1, 1))
    return left + right


def row_sides(f, low, high):
    row = iota(f.shape, 0)
    below = jnp.where(row == 0, low, pltpu.roll(f, 1, 0))
    above = jnp.where(row == CY - 1, high, pltpu.roll(f, CY - 1, 0))
    return below + above


def products_t(picked, blocks, first):
    row = iota((8, LANES), 0)
    out = []
    for q in range(picked.shape[0] // 8):
        p = picked[8 * q : 8 * q + 8, :]
        lhs = jnp.concatenate([jnp.where(row == i, p, 0.0) for i in range(8)], axis=1)
        at = first + 8 * q
        out.append(dot(lhs.astype(BF16), blocks[at : at + 8].reshape(8 * LANES, LANES), 1, 0))
    return jnp.concatenate(out, axis=0)


def products(x, blocks, r_hot):
    row = iota((8, LANES), 0)
    out = []
    for q in range(SLOTS // 8):
        p = x[8 * q : 8 * q + 8, :]
        lhs = jnp.concatenate([jnp.where(row == i, p, 0.0) for i in range(8)], axis=1)
        rhs = jnp.concatenate([blocks[8 * q + i] for i in range(8)], axis=1)
        out.append(dot(lhs.astype(BF16), rhs, 1, 1))
    return onehot_dot(r_hot, jnp.concatenate(out, axis=0), 1, 0)


def edge_tiles(scratch, low, high, scalar):
    for x in range(CX):
        scratch[0, x : x + 1, :] = low[x]
        scratch[1, x : x + 1, :] = high[x]
    for i, term in enumerate(terms(scalar)):
        scratch[0, CX + i : CX + i + 1, :] = wide(term)
        scratch[1, CX + i : CX + i + 1, :] = wide(term)
    scratch[0, 7:8, :] = jnp.zeros((1, LANES), F32)
    scratch[1, 7:8, :] = jnp.zeros((1, LANES), F32)
    return scratch[0], scratch[1]


def kernel_index(cols, rows, count, p_out, p_wide_out, r_out, note_out):
    col = cols[...]
    live = iota((1, SLOTS), 1) < count[...]
    slab = RAY * CY
    owner = lax.div(lax.rem(col, slab), CY)
    local = lax.div(col, slab) * CY + lax.rem(col, CY)
    own_hot = iota((RAY, SLOTS), 0) == owner
    before = (iota((SLOTS, SLOTS), 0) < iota((SLOTS, SLOTS), 1)).astype(F32).astype(BF16)
    earlier = dot(own_hot.astype(F32).astype(BF16), before, 1, 0)
    rank = jnp.sum(jnp.where(own_hot, earlier, 0.0), axis=0, keepdims=True).astype(jnp.int32)
    p_f = ((iota((RAY * CAP, SLOTS), 0) == owner * CAP + rank) & live).astype(F32)
    p_out[...] = p_f.astype(BF16)
    p_wide_out[...] = ((iota((RAY * MSG, SLOTS), 0) == owner * MSG + rank) & live).astype(F32).astype(BF16)
    r_out[...] = ((iota((KB, SLOTS), 0) == rows[...]) & live).astype(F32).astype(BF16)
    ids = jnp.sum(p_f * (local + 1).astype(F32), axis=1, keepdims=True) - 1.0
    note_out[...] = jnp.broadcast_to(ids, (RAY * CAP, LANES))


def kernel_start(pos_ref, start, note, blocks, p_hot, r_hot, send):
    data = start[:, 0:KOWN, :].reshape(KB, LANES)
    contrib = products_t(dot(r_hot[...], data.astype(BF16), 0, 0), blocks, 0)
    send[:, 0:CAP, :] = onehot_dot(p_hot[...], contrib, 1, 0).reshape(RAY, CAP, LANES)
    lane = iota((RAY * CAP, LANES), 1)
    send[:, CAP:MSG, :] = jnp.where(lane < LANES // 2, note[...], total(data * data)).reshape(RAY, CAP, LANES)


def send_columns(send, q_hot, v_raw, scratch, low, high, scalar, ray):
    columns = dot(q_hot, v_raw.astype(BF16), 1, 0)
    low, high = edge_tiles(scratch, low, high, scalar)
    for d in range(RAY):
        edge = jnp.where(d > ray, high, low)
        send[d] = jnp.concatenate([columns[CAP * d : CAP * d + CAP], edge], axis=0).astype(BF16)


def kernel_first_v(pos_ref, recv, send, v_out, q_out, beta_out, scratch):
    contrib = recv[:, 0:CAP, :].reshape(RAY * CAP, LANES)
    note = recv[:, CAP:MSG, :].reshape(RAY * CAP, LANES)
    lane = iota((RAY * CAP, LANES), 1)
    row = iota((RAY * CAP, LANES), 0)
    q_hot = (note[:, 0:CELLS] == iota((RAY * CAP, CELLS), 1).astype(F32)).astype(F32).astype(BF16)
    q_out[...] = q_hot
    squares = total(jnp.where((lane == LANES - 1) & (lax.rem(row, CAP) == 0), note, 0.0))
    beta = jnp.sqrt(squares + eps)
    beta_out[...] = wide(beta)
    v_raw = onehot_dot(q_hot, contrib, 0, 0) / beta
    v_out[...] = v_raw
    low = [v_raw[CY * x : CY * x + 1, :] for x in range(CX)]
    high = [v_raw[CY * x + CY - 1 : CY * x + CY, :] for x in range(CX)]
    send_columns(send, q_hot, v_raw, scratch, low, high, total(v_raw * v_raw), pos_ref[0])


def kernel_forward(pos_ref, recv, p_wide, r_hot, blocks, v_raw, send, scratch):
    ray = pos_ref[0]
    x = dot(p_wide[...], recv[...].reshape(RAY * MSG, LANES), 0, 0)
    part = products(x, blocks, r_hot[...]).astype(BF16)
    norm = jnp.zeros((MSG, LANES), F32)
    for d in range(RAY):
        norm = norm + recv[d].astype(F32)
    low = recv[jnp.maximum(ray - 1, 0)].astype(F32)
    high = recv[jnp.minimum(ray + 1, RAY - 1)].astype(F32)
    scratch[0:CX, :] = jnp.where(ray > 0, low[CAP : CAP + CX], 0.0)
    scratch[CX : 2 * CX, :] = jnp.where(ray < RAY - 1, high[CAP : CAP + CX], 0.0)
    at = CAP + CX
    norm = norm[at : at + 1] + (norm[at + 1 : at + 2] + norm[at + 2 : at + 3])
    for i, term in enumerate(terms(norm)):
        scratch[2 * CX + i : 2 * CX + i + 1, :] = term
    scratch[2 * CX + 3 : 16, :] = jnp.zeros((16 - 2 * CX - 3, LANES), F32)
    edge = scratch[...].astype(BF16)
    mine = v_raw[...].astype(BF16)
    for t in range(TILE):
        send[t, 0:KB, :] = part
        send[t, KB : KB + CELLS, :] = mine
        send[t, KB + CELLS : TMSG, :] = edge


def gathered(recv, v_raw, tile, slab, edges):
    kv = recv[0, 0:KB, :].astype(F32)
    for t in range(1, TILE):
        kv = kv + recv[t, 0:KB, :].astype(F32)
    slab[0] = jnp.zeros((CY, LANES), F32)
    slab[XS + 1] = jnp.zeros((CY, LANES), F32)
    norm = jnp.zeros((8, LANES), F32)
    for t in range(TILE):
        for h in range(CELLS // 16):
            both = recv[t, KB + 16 * h : KB + 16 * h + 16, :].astype(F32)
            slab[CX * t + 2 * h + 1] = both[0:CY]
            slab[CX * t + 2 * h + 2] = both[CY : 2 * CY]
        edge = recv[t, KB + CELLS : TMSG, :].astype(F32)
        edges[t] = edge[0:8]
        norm = norm + edge[8:16]
    for x in range(CX):
        slab[CX * tile + x + 1] = v_raw[CY * x : CY * x + CY, :]
    return kv, jnp.sqrt(norm[0:1] + (norm[1:2] + norm[2:3]) + eps)


def slab_laplace(slab, edges, index):
    t, x = divmod(index, CX)
    f = slab[index + 1]
    beside = row_sides(f, edges[t, x : x + 1, :], edges[t, CX + x : CX + x + 1, :])
    beside = beside + lane_sides(f) + slab[index] + slab[index + 2]
    return 6.0 * f - beside


def cell_weight(start, index):
    t, x = divmod(index, CX)
    return start[t, KOWN + CY * x : KOWN + CY * x + CY, :]


def kernel_back(
    pos_ref, recv, v_raw, start, beta0, blocks, p_hot, r_hot,
    send, raw1_out, raw2_out, alpha_out, nq_out,
    scratch, slab, edges, field,
):
    ray, tile = pos_ref[0], pos_ref[1]
    kv, alpha = gathered(recv, v_raw, tile, slab, edges)
    alpha_out[...] = alpha
    raw1 = kv / alpha - alpha * (start[:, 0:KOWN, :].reshape(KB, LANES) / beta0[...])
    raw1_out[...] = raw1
    field[0] = jnp.zeros((CY, LANES), F32)
    field[XS + 1] = jnp.zeros((CY, LANES), F32)
    squares = jnp.zeros((CY, LANES), F32)
    for i in range(XS):
        weight = cell_weight(start, i)
        raw2 = weight * (slab_laplace(slab, edges, i) / alpha)
        raw2_out[i] = raw2
        squares = squares + raw2 * raw2
        field[i + 1] = weight * raw2
    contrib = products_t(dot(r_hot[...], raw1.astype(BF16), 0, 0), blocks, 0)
    send[:, 0:CAP, :] = onehot_dot(p_hot[...], contrib, 1, 0).reshape(RAY, CAP, LANES)
    low, high = [], []
    for x in range(CX):
        at = tile * CX + x + 1
        f = field[at]
        beside = row_sides(f, 0.0, 0.0) + lane_sides(f) + field[at - 1] + field[at + 1]
        nq_out[CY * x : CY * x + CY, :] = 6.0 * f - beside
        low.append(f[0:1])
        high.append(f[CY - 1 : CY])
    low, high = edge_tiles(scratch, low, high, total(raw1 * raw1) + total(squares))
    for d in range(RAY):
        send[d, CAP:MSG, :] = jnp.where(d > ray, high, low)


def kernel_next_v(pos_ref, recv, q_ref, v0_raw, alpha0, nq, send, v_out, beta_out, scratch):
    ray = pos_ref[0]
    contrib = recv[:, 0:CAP, :].reshape(RAY * CAP, LANES)
    q_hot = q_ref[...]
    norm = recv[0, CAP:MSG, :]
    for d in range(1, RAY):
        norm = norm + recv[d, CAP:MSG, :]
    beta = jnp.sqrt(norm[CX : CX + 1] + (norm[CX + 1 : CX + 2] + norm[CX + 2 : CX + 3]) + eps)
    beta_out[...] = beta
    z = onehot_dot(q_hot, contrib, 0, 0)
    low = jnp.where(ray > 0, recv[jnp.maximum(ray - 1, 0), CAP:MSG, :], 0.0)
    high = jnp.where(ray < RAY - 1, recv[jnp.minimum(ray + 1, RAY - 1), CAP:MSG, :], 0.0)
    row = iota((CY, LANES), 0)
    squares = jnp.zeros((CY, LANES), F32)
    edges_low, edges_high, parts = [], [], []
    for x in range(CX):
        cut = slice(CY * x, CY * x + CY)
        edge = jnp.where(row == 0, low[x : x + 1], 0.0) + jnp.where(row == CY - 1, high[x : x + 1], 0.0)
        v_raw = (z[cut] + (nq[cut, :] - edge)) / beta - beta * (v0_raw[cut, :] / alpha0[...])
        v_out[cut, :] = v_raw
        parts.append(v_raw)
        squares = squares + v_raw * v_raw
        edges_low.append(v_raw[0:1])
        edges_high.append(v_raw[CY - 1 : CY])
    send_columns(send, q_hot, jnp.concatenate(parts, axis=0), scratch, edges_low, edges_high, total(squares), ray)


def kernel_last_norm(
    pos_ref, recv, v_raw, start, beta1, raw1_ref, raw2_ref, send, raw1_out, alpha_out, scratch, slab, edges
):
    tile = pos_ref[1]
    kv, alpha = gathered(recv, v_raw, tile, slab, edges)
    alpha_out[...] = alpha
    raw1 = kv / alpha - alpha * (raw1_ref[...] / beta1[...])
    scratch[...] = raw1.reshape(TILE, KOWN, LANES)
    raw1_out[...] = scratch[tile]
    squares = jnp.zeros((CY, LANES), F32)
    for i in range(XS):
        raw2 = cell_weight(start, i) * (slab_laplace(slab, edges, i) / alpha) - alpha * (raw2_ref[i] / beta1[...])
        squares = squares + raw2 * raw2
    norm = total(raw1 * raw1) + total(squares)
    send[...] = jnp.broadcast_to(norm.reshape(1, 1, 1), (RAY, 1, LANES))


def kernel_end(recv, v0_raw, v1_raw, raw1, beta0, beta1, alpha0, alpha1, model_out, u_out):
    norm = recv[0]
    for d in range(1, RAY):
        norm = norm + recv[d]
    b0, b1, b2 = beta0[...], beta1[...], jnp.sqrt(norm + eps)
    a0, a1 = alpha0[...], alpha1[...]
    v0, v1 = v0_raw[...] / a0, v1_raw[...] / a1
    rho1 = jnp.sqrt(a0 * a0 + b1 * b1)
    cosine1, sine1 = a0 / rho1, b1 / rho1
    theta = sine1 * a1
    rhobar = -cosine1 * a1
    phi1, phibar = cosine1 * b0, sine1 * b0
    w1 = v1 - theta / rho1 * v0
    rho2 = jnp.sqrt(rhobar * rhobar + b2 * b2)
    phi2 = rhobar / rho2 * phibar
    model_out[...] = phi1 / rho1 * v0 + phi2 / rho2 * w1
    u_out[...] = raw1[...] / b2


VM = pl.BlockSpec(memory_space=pltpu.VMEM)
SM = pl.BlockSpec(memory_space=pltpu.SMEM)


def call(kernel, outs, args, specs=None, scratch=()):
    return pl.pallas_call(
        kernel,
        out_shape=[jax.ShapeDtypeStruct(shape, kind) for shape, kind in outs],
        in_specs=specs or [SM] + [VM] * (len(args) - 1),
        out_specs=[VM] * len(outs),
        scratch_shapes=[pltpu.VMEM(s, F32) if isinstance(s, tuple) else s for s in scratch],
        compiler_params=pltpu.CompilerParams(vmem_limit_bytes=32 * 2**20),
        name=kernel.__name__,
    )(*args)


def shards(data, blocks, block_cols, block_rows, block_counts, reg_weight):
    pos = jnp.stack([lax.axis_index("ray"), lax.axis_index("tile")]).astype(jnp.int32)
    weight = reg_weight.reshape(CELLS, LANES)
    message = ((RAY, MSG, LANES), F32)
    half_message = ((RAY, MSG, LANES), BF16)
    tile_message = ((TILE, TMSG, LANES), BF16)
    scalar = ((1, LANES), F32)
    cells = ((CELLS, LANES), F32)
    rays = ((KB, LANES), F32)
    slab = ((XS, CY, LANES), F32)
    edges = (2, 8, LANES)
    slabs = [(XS + 2, CY, LANES), (TILE, 8, LANES)]
    own = jnp.concatenate([data.reshape(KOWN, LANES), weight], axis=0)
    start = lax.all_to_all(jnp.broadcast_to(own, (TILE,) + own.shape), "tile", 0, 0)
    p_hot, p_wide, r_hot, note = call(
        kernel_index,
        [
            ((RAY * CAP, SLOTS), BF16),
            ((RAY * MSG, SLOTS), BF16),
            ((KB, SLOTS), BF16),
            ((RAY * CAP, LANES), F32),
        ],
        (block_cols[0], block_rows[0], block_counts),
        [VM] * 3,
    )
    values = blocks[0, 0]
    (send,) = call(kernel_start, [message], (pos, start, note, values, p_hot, r_hot))
    recv = lax.all_to_all(send, "ray", 0, 0)
    send, v0_raw, q_hot, beta0 = call(
        kernel_first_v,
        [half_message, cells, ((RAY * CAP, CELLS), BF16), scalar],
        (pos, recv),
        scratch=[edges],
    )
    recv = lax.all_to_all(send, "ray", 0, 0)
    (send,) = call(
        kernel_forward, [tile_message], (pos, recv, p_wide, r_hot, values, v0_raw), scratch=[(16, LANES)]
    )
    recv = lax.all_to_all(send, "tile", 0, 0)
    send, raw1, raw2, alpha0, nq = call(
        kernel_back,
        [message, rays, slab, scalar, cells],
        (pos, recv, v0_raw, start, beta0, values, p_hot, r_hot),
        scratch=[edges] + slabs + slabs[:1],
    )
    recv = lax.all_to_all(send, "ray", 0, 0)
    send, v1_raw, beta1 = call(
        kernel_next_v,
        [half_message, cells, scalar],
        (pos, recv, q_hot, v0_raw, alpha0, nq),
        scratch=[edges],
    )
    recv = lax.all_to_all(send, "ray", 0, 0)
    (send,) = call(
        kernel_forward, [tile_message], (pos, recv, p_wide, r_hot, values, v1_raw), scratch=[(16, LANES)]
    )
    recv = lax.all_to_all(send, "tile", 0, 0)
    send, raw1_own, alpha1 = call(
        kernel_last_norm,
        [((RAY, 1, LANES), F32), ((KOWN, LANES), F32), scalar],
        (pos, recv, v1_raw, start, beta1, raw1, raw2),
        scratch=[(TILE, KOWN, LANES)] + slabs,
    )
    recv = lax.all_to_all(send, "ray", 0, 0)
    model, rays = call(
        kernel_end,
        [cells, ((KOWN, LANES), F32)],
        (recv, v0_raw, v1_raw, raw1_own, beta0, beta1, alpha0, alpha1),
        [VM] * 8,
    )
    return model.reshape(reg_weight.shape), rays.reshape(data.shape)


def solution(mesh):
    return jax.shard_map(
        shards,
        mesh=mesh,
        in_specs=(
            P(("ray", "tile")),
            P("ray", "tile", None, None, None),
            P("ray", "tile", None),
            P("ray", "tile", None),
            P("ray", "tile"),
            P("tile", "ray", None),
        ),
        out_specs=(P("tile", "ray", None), P(("ray", "tile"))),
        check_vma=False,
    )
```

time: 139 us -> 124 us (0.89)
  blocking collectives: 104 us -> 91.9 us
  waiting for transfers between devices: 7.42 us -> 5.81 us
    all_to_all x2, blocking collectives: 38 us -> 27.9 us  [shards(): recv = lax.all_to_all(send, 'tile', 0, 0)]
    all_to_all x5, blocking collectives: 66.4 us -> 64 us  [shards(): recv = lax.all_to_all(send, 'ray', 0, 0)]
    all_to_all x1, waiting for transfers between devices: 7.42 us -> 5.81 us  [shards(): lax.all_to_all(jnp.broadcast_to(own, (TILE,) + own.shape), 'tile', 0, 0)]
    pallas_call x8 -> x9, Pallas kernels: 10.9 us -> 10.9 us  [call(): pl.pallas_call(kernel, out_shape=[jax.ShapeDtypeStruct(shape, kind) for s...]
where the time goes in v2:
time: 124 us
  blocking collectives  91.9 us (74%)
  Pallas kernels  10.9 us (9%)
  starting transfers between devices  9.01 us (7%)
  waiting for transfers between devices  5.81 us (5%)
  local copies, waits for them, and re-layouts  4.17 us (3%)
  between operations  1.36 us (1%)
    all_to_all x5, blocking collectives, shards(): recv = lax.all_to_all(send, 'ray', 0, 0)  64 us
    all_to_all x2, blocking collectives, shards(): recv = lax.all_to_all(send, 'tile', 0, 0)  27.9 us
    pallas_call x9, Pallas kernels, call(): pl.pallas_call(kernel, out_shape=[jax.ShapeDtypeStruct(shape, kind) for s...  10.9 us
    all_to_all x1, starting transfers between devices, shards(): lax.all_to_all(jnp.broadcast_to(own, (TILE,) + own.shape), 'tile', 0, 0)  9.01 us
    all_to_all x1, waiting for transfers between devices, shards(): lax.all_to_all(jnp.broadcast_to(own, (TILE,) + own.shape), 'tile', 0, 0)  5.81 us
    unnamed x8, local copies, waits for them, and re-layouts  3.5 us
  transfers between devices with their start and end apart: 1, of which 1 were waited for; matrix products, arithmetic and copies ran while one was open for 0% of the time, Pallas kernels for 0%

profile of v2, /device:TPU:1, one launch (start us, length us, event | category | flops | bytes accessed | tf_op | source)
XLA Modules:
  0.0 123.9 jit_solution(755925115389862679)
XLA Ops:
  0.6 0.7 pad_maximum_fusion
  1.4 0.7 broadcast_in_dim.3
  2.0 9.0 %all-to-all-start = ((f32[8,40,128]{2,1,0:T(8,128)}), f32[8,40,128]{2,1,0:T(8,128)S(1)}, u32[]{:S(2)}, u32[]{:S(2)}) async-start(f32[8,40,128]{2,1,0:T(8,128)} %broadcast_in_dim.3), calls=%async_computation | async-start | bytes 327680 | tf_op jit(solution)/shard_map/all_to_all | solution.py:340
  11.7 0.0 copy-start.2
  11.7 0.6 copy-done.2
  12.4 0.0 copy-start.3
  12.4 0.7 copy-done.3
  13.0 0.3 kernel_index.1
  13.3 0.1 pad_add_fusion.pos_ref
  13.4 5.8 %all-to-all-done.start = f32[8,40,128]{2,1,0:T(8,128)S(1)} async-done(((f32[8,40,128]{2,1,0:T(8,128)}), f32[8,40,128]{2,1,0:T(8,128)S(1)}, u32[]{:S(2)}, u32[]{:S(2)}) %all-to-all-start) | async-done | bytes 163872 | tf_op jit(solution)/shard_map/all_to_all | solution.py:340
  19.2 0.0 copy-start
  19.2 2.2 %copy-done = bf16[1,1,128,128,128]{4,3,2,1,0:T(8,128)(2,1)S(1)} copy-done((bf16[1,1,128,128,128]{4,3,2,1,0:T(8,128)(2,1)S(1)}, bf16[1,1,128,128,128]{4,3,2,1,0:T(8,128)(2,1)}, u32[]{:S(2)}) %copy-start) | copy-done | bytes 4194328
  21.4 0.0 copy-start.1
  21.4 1.5 %kernel_start.1 = f32[32,16,128]{2,1,0:T(8,128)S(1)} custom-call(s32[2]{0:T(128)S(1)} %pad_add_fusion.pos_ref, f32[8,40,128]{2,1,0:T(8,128)S(1)} %all-to-all-done.start, f32[256,128]{1,0:T(8,128)S(1)} %get-tuple-element.23.note, bf16[128,128,128]{2,1,0:T(8,128)(2,1)S(1)} %bitcast.9, bf16[256,128]{1,0:T(8,128)(2,1)S(1)} %get-tuple-element.24.p_hot, ...), custom_call_target="tpu_custom_call" | custom-call | tf_op jit(solution)/shard_map/kernel_start/pallas_call | solution.py:316
  22.9 18.4 %all_to_all.40.recv = f32[32,16,128]{2,1,0:T(8,128)S(1)} all-to-all(f32[32,16,128]{2,1,0:T(8,128)S(1)} %kernel_start.1), channel_id=1, replica_groups=mesh['ray'=32,'tile'=8] {'ray'}, dimensions={0} | all-to-all | bytes 524288 | tf_op jit(solution)/shard_map/all_to_all | solution.py:354
  41.4 0.9 kernel_first_v.1
  42.3 11.2 %all_to_all.41.recv = bf16[32,16,128]{2,1,0:T(8,128)(2,1)S(1)} all-to-all(bf16[32,16,128]{2,1,0:T(8,128)(2,1)S(1)} %get-tuple-element.26), channel_id=1, replica_groups=mesh['ray'=32,'tile'=8] {'ray'}, dimensions={0} | all-to-all | bytes 262144 | tf_op jit(solution)/shard_map/all_to_all | solution.py:361
  53.5 0.0 copy-done.1
  53.5 2.1 %kernel_forward.2 = bf16[8,112,128]{2,1,0:T(8,128)(2,1)S(1)} custom-call(s32[2]{0:T(128)S(1)} %pad_add_fusion.pos_ref, bf16[32,16,128]{2,1,0:T(8,128)(2,1)S(1)} %all_to_all.41.recv, bf16[512,128]{1,0:T(8,128)(2,1)S(1)} %get-tuple-element.27.p_wide, bf16[64,128]{1,0:T(8,128)(2,1)S(1)} %get-tuple-element.25.r_hot, bf16[128,128,128]{2,1,0:T(8,128)(2,1)S(1)} %bitcast.10, ...), custom_call_target="tpu_custom_call" | custom-call | tf_op jit(solution)/shard_map/kernel_forward/pallas_call | solution.py:316
  55.6 13.9 %all_to_all.42.recv = bf16[8,112,128]{2,1,0:T(8,128)(2,1)S(1)} all-to-all(bf16[8,112,128]{2,1,0:T(8,128)(2,1)S(1)} %kernel_forward.2), channel_id=1, replica_groups=mesh['ray'=32,'tile'=8] {'tile'}, dimensions={0} | all-to-all | bytes 458752 | tf_op jit(solution)/shard_map/all_to_all | solution.py:365
  69.5 1.6 %kernel_back.1 = (f32[32,16,128]{2,1,0:T(8,128)S(1)}, f32[64,128]{1,0:T(8,128)S(1)}, f32[32,8,128]{2,1,0:T(8,128)S(1)}, f32[1,128]{1,0:T(1,128)S(1)}, f32[32,128]{1,0:T(8,128)S(1)}) custom-call(s32[2]{0:T(128)S(1)} %pad_add_fusion.pos_ref, bf16[8,112,128]{2,1,0:T(8,128)(2,1)S(1)} %all_to_all.42.recv, f32[32,128]{1,0:T(8,128)S(1)} %get-tuple-element.28.v_raw.v0_raw, ...), custom_call_target="tpu_custom_call" | custom-call | tf_op jit(solution)/shard_map/kernel_back/pallas_call | solution.py:316
  71.1 12.6 %all_to_all.43.recv = f32[32,16,128]{2,1,0:T(8,128)S(1)} all-to-all(f32[32,16,128]{2,1,0:T(8,128)S(1)} %get-tuple-element.30), channel_id=1, replica_groups=mesh['ray'=32,'tile'=8] {'ray'}, dimensions={0} | all-to-all | bytes 524288 | tf_op jit(solution)/shard_map/all_to_all | solution.py:372
  83.7 0.9 kernel_next_v.1
  84.6 11.2 %all_to_all.44.recv = bf16[32,16,128]{2,1,0:T(8,128)(2,1)S(1)} all-to-all(bf16[32,16,128]{2,1,0:T(8,128)(2,1)S(1)} %get-tuple-element.34), channel_id=1, replica_groups=mesh['ray'=32,'tile'=8] {'ray'}, dimensions={0} | all-to-all | bytes 262144 | tf_op jit(solution)/shard_map/all_to_all | solution.py:379
  95.8 2.1 %kernel_forward.3 = bf16[8,112,128]{2,1,0:T(8,128)(2,1)S(1)} custom-call(s32[2]{0:T(128)S(1)} %pad_add_fusion.pos_ref, bf16[32,16,128]{2,1,0:T(8,128)(2,1)S(1)} %all_to_all.44.recv, bf16[512,128]{1,0:T(8,128)(2,1)S(1)} %get-tuple-element.27.p_wide, bf16[64,128]{1,0:T(8,128)(2,1)S(1)} %get-tuple-element.25.r_hot, bf16[128,128,128]{2,1,0:T(8,128)(2,1)S(1)} %bitcast.12, ...), custom_call_target="tpu_custom_call" | custom-call | tf_op jit(solution)/shard_map/kernel_forward/pallas_call | solution.py:316
  97.9 13.9 %all_to_all.45.recv = bf16[8,112,128]{2,1,0:T(8,128)(2,1)S(1)} all-to-all(bf16[8,112,128]{2,1,0:T(8,128)(2,1)S(1)} %kernel_forward.3), channel_id=1, replica_groups=mesh['ray'=32,'tile'=8] {'tile'}, dimensions={0} | all-to-all | bytes 458752 | tf_op jit(solution)/shard_map/all_to_all | solution.py:383
  111.9 0.8 kernel_last_norm.1
  112.7 10.6 %all_to_all.46.recv = f32[32,1,128]{2,1,0:T(1,128)S(1)} all-to-all(f32[32,1,128]{2,1,0:T(1,128)S(1)} %get-tuple-element.39), channel_id=1, replica_groups=mesh['ray'=32,'tile'=8] {'ray'}, dimensions={0} | all-to-all | bytes 32768 | tf_op jit(solution)/shard_map/all_to_all | solution.py:390
  123.2 0.7 kernel_end.1
Async XLA Ops:
  2.0 17.2 %all-to-all-start = ((f32[8,40,128]{2,1,0:T(8,128)}), f32[8,40,128]{2,1,0:T(8,128)S(1)}, u32[]{:S(2)}, u32[]{:S(2)}) async-start(f32[8,40,128]{2,1,0:T(8,128)} %broadcast_in_dim.3), calls=%async_computation | async-start | bytes 327680 | tf_op jit(solution)/shard_map/all_to_all | solution.py:340
  11.7 0.7 copy-start.2
  12.4 0.7 copy-start.3
  19.2 2.2 %copy-start = (bf16[1,1,128,128,128]{4,3,2,1,0:T(8,128)(2,1)S(1)}, bf16[1,1,128,128,128]{4,3,2,1,0:T(8,128)(2,1)}, u32[]{:S(2)}) copy-start(bf16[1,1,128,128,128]{4,3,2,1,0:T(8,128)(2,1)} %param.7) | copy-start | bytes 12582916
  21.4 32.1 %copy-start.1 = (bf16[1,1,128,128,128]{4,3,2,1,0:T(8,128)(2,1)S(1)}, bf16[1,1,128,128,128]{4,3,2,1,0:T(8,128)(2,1)}, u32[]{:S(2)}) copy-start(bf16[1,1,128,128,128]{4,3,2,1,0:T(8,128)(2,1)} %param.7) | copy-start | bytes 12582916

commit v3 on v2

--- a/solution.py
+++ b/solution.py
@@ -18,6 +18,7 @@
 MSG = 2 * CAP
 TMSG = KB + CELLS + 16
 SMSG = KOWN + CELLS
+CHUNKS = 4
 XS = TILE * CX
 eps = 1e-06
 
@@ -103,7 +104,7 @@
     return scratch[0], scratch[1]
 
 
-def kernel_index(cols, rows, count, p_out, p_wide_out, r_out, note_out):
+def kernel_index(cols, rows, count, p_out, p_wide_out, r_out, r_turned_out, note_out):
     col = cols[...]
     live = iota((1, SLOTS), 1) < count[...]
     slab = RAY * CY
@@ -115,18 +116,49 @@
     rank = jnp.sum(jnp.where(own_hot, earlier, 0.0), axis=0, keepdims=True).astype(jnp.int32)
     p_f = ((iota((RAY * CAP, SLOTS), 0) == owner * CAP + rank) & live).astype(F32)
     p_out[...] = p_f.astype(BF16)
-    p_wide_out[...] = ((iota((RAY * MSG, SLOTS), 0) == owner * MSG + rank) & live).astype(F32).astype(BF16)
-    r_out[...] = ((iota((KB, SLOTS), 0) == rows[...]) & live).astype(F32).astype(BF16)
+    p_wide = ((iota((RAY * MSG, SLOTS), 0) == owner * MSG + rank) & live).astype(F32)
+    p_wide_out[...] = p_wide.T.astype(BF16)
+    r_f = ((iota((KB, SLOTS), 0) == rows[...]) & live).astype(F32)
+    r_out[...] = r_f.astype(BF16)
+    r_turned_out[...] = r_f.T.astype(BF16)
     ids = jnp.sum(p_f * (local + 1).astype(F32), axis=1, keepdims=True) - 1.0
     note_out[...] = jnp.broadcast_to(ids, (RAY * CAP, LANES))
 
 
-def kernel_start(pos_ref, start, note, blocks, p_hot, r_hot, send):
+def send_contributions(send, p_hot, contrib, notes):
+    slots = dot(p_hot, contrib.astype(BF16), 1, 0)
+    for d in range(RAY):
+        send[d] = jnp.concatenate([slots[CAP * d : CAP * d + CAP], notes(d)], axis=0).astype(BF16)
+
+
+def received(recv):
+    both = [recv[d].astype(F32) for d in range(RAY)]
+    contrib = jnp.concatenate([x[0:CAP] for x in both], axis=0).astype(BF16)
+    return contrib, [x[CAP:MSG] for x in both]
+
+
+def kernel_start(pos_ref, start, note, blocks, p_hot, r_turned, send, held, sems):
+    per = SLOTS // CHUNKS
+    copies = [
+        pltpu.make_async_copy(blocks.at[pl.ds(c * per, per)], held.at[pl.ds(c * per, per)], sems.at[c])
+        for c in range(CHUNKS)
+    ]
+    for copy in copies:
+        copy.start()
     data = start[:, 0:KOWN, :].reshape(KB, LANES)
-    contrib = products_t(dot(r_hot[...], data.astype(BF16), 0, 0), blocks, 0)
-    send[:, 0:CAP, :] = onehot_dot(p_hot[...], contrib, 1, 0).reshape(RAY, CAP, LANES)
-    lane = iota((RAY * CAP, LANES), 1)
-    send[:, CAP:MSG, :] = jnp.where(lane < LANES // 2, note[...], total(data * data)).reshape(RAY, CAP, LANES)
+    picked = dot(r_turned[...], data.astype(BF16), 1, 0)
+    contrib = []
+    for c, copy in enumerate(copies):
+        copy.wait()
+        contrib.append(products_t(picked[c * per : (c + 1) * per], held, c * per))
+    contrib = jnp.concatenate(contrib, axis=0)
+    quarter = iota((CAP, LANES), 1) // CELLS
+    high, mid, low = terms(total(data * data))
+    squares = jnp.where(quarter == 1, high, jnp.where(quarter == 2, mid, low))
+    send_contributions(
+        send, p_hot[...], contrib,
+        lambda d: jnp.where(quarter == 0, note[CAP * d : CAP * d + CAP, :], squares),
+    )
 
 
 def send_columns(send, q_hot, v_raw, scratch, low, high, scalar, ray):
@@ -138,16 +170,18 @@
 
 
 def kernel_first_v(pos_ref, recv, send, v_out, q_out, beta_out, scratch):
-    contrib = recv[:, 0:CAP, :].reshape(RAY * CAP, LANES)
-    note = recv[:, CAP:MSG, :].reshape(RAY * CAP, LANES)
-    lane = iota((RAY * CAP, LANES), 1)
-    row = iota((RAY * CAP, LANES), 0)
+    contrib, notes = received(recv)
+    norm = notes[0][0:1]
+    for d in range(1, RAY):
+        norm = norm + notes[d][0:1]
+    note = jnp.concatenate(notes, axis=0)
     q_hot = (note[:, 0:CELLS] == iota((RAY * CAP, CELLS), 1).astype(F32)).astype(F32).astype(BF16)
     q_out[...] = q_hot
-    squares = total(jnp.where((lane == LANES - 1) & (lax.rem(row, CAP) == 0), note, 0.0))
+    lane = iota((1, LANES), 1)
+    squares = total(jnp.where((lane > 0) & (lane % CELLS == 0), norm, 0.0))
     beta = jnp.sqrt(squares + eps)
     beta_out[...] = wide(beta)
-    v_raw = onehot_dot(q_hot, contrib, 0, 0) / beta
+    v_raw = dot(q_hot, contrib, 0, 0) / beta
     v_out[...] = v_raw
     low = [v_raw[CY * x : CY * x + 1, :] for x in range(CX)]
     high = [v_raw[CY * x + CY - 1 : CY * x + CY, :] for x in range(CX)]
@@ -156,7 +190,7 @@
 
 def kernel_forward(pos_ref, recv, p_wide, r_hot, blocks, v_raw, send, scratch):
     ray = pos_ref[0]
-    x = dot(p_wide[...], recv[...].reshape(RAY * MSG, LANES), 0, 0)
+    x = dot(p_wide[...], recv[...].reshape(RAY * MSG, LANES), 1, 0)
     part = products(x, blocks, r_hot[...]).astype(BF16)
     norm = jnp.zeros((MSG, LANES), F32)
     for d in range(RAY):
@@ -212,7 +246,7 @@
 
 
 def kernel_back(
-    pos_ref, recv, v_raw, start, beta0, blocks, p_hot, r_hot,
+    pos_ref, recv, v_raw, start, beta0, blocks, p_hot, r_turned,
     send, raw1_out, raw2_out, alpha_out, nq_out,
     scratch, slab, edges, field,
 ):
@@ -230,8 +264,7 @@
         raw2_out[i] = raw2
         squares = squares + raw2 * raw2
         field[i + 1] = weight * raw2
-    contrib = products_t(dot(r_hot[...], raw1.astype(BF16), 0, 0), blocks, 0)
-    send[:, 0:CAP, :] = onehot_dot(p_hot[...], contrib, 1, 0).reshape(RAY, CAP, LANES)
+    contrib = products_t(dot(r_turned[...], raw1.astype(BF16), 1, 0), blocks, 0)
     low, high = [], []
     for x in range(CX):
         at = tile * CX + x + 1
@@ -241,22 +274,21 @@
         low.append(f[0:1])
         high.append(f[CY - 1 : CY])
     low, high = edge_tiles(scratch, low, high, total(raw1 * raw1) + total(squares))
-    for d in range(RAY):
-        send[d, CAP:MSG, :] = jnp.where(d > ray, high, low)
+    send_contributions(send, p_hot[...], contrib, lambda d: jnp.where(d > ray, high, low))
 
 
 def kernel_next_v(pos_ref, recv, q_ref, v0_raw, alpha0, nq, send, v_out, beta_out, scratch):
     ray = pos_ref[0]
-    contrib = recv[:, 0:CAP, :].reshape(RAY * CAP, LANES)
+    contrib, notes = received(recv)
     q_hot = q_ref[...]
-    norm = recv[0, CAP:MSG, :]
+    norm = notes[0]
     for d in range(1, RAY):
-        norm = norm + recv[d, CAP:MSG, :]
+        norm = norm + notes[d]
     beta = jnp.sqrt(norm[CX : CX + 1] + (norm[CX + 1 : CX + 2] + norm[CX + 2 : CX + 3]) + eps)
     beta_out[...] = beta
-    z = onehot_dot(q_hot, contrib, 0, 0)
-    low = jnp.where(ray > 0, recv[jnp.maximum(ray - 1, 0), CAP:MSG, :], 0.0)
-    high = jnp.where(ray < RAY - 1, recv[jnp.minimum(ray + 1, RAY - 1), CAP:MSG, :], 0.0)
+    z = dot(q_hot, contrib, 0, 0)
+    low = jnp.where(ray > 0, recv[jnp.maximum(ray - 1, 0)].astype(F32)[CAP:MSG], 0.0)
+    high = jnp.where(ray < RAY - 1, recv[jnp.minimum(ray + 1, RAY - 1)].astype(F32)[CAP:MSG], 0.0)
     row = iota((CY, LANES), 0)
     squares = jnp.zeros((CY, LANES), F32)
     edges_low, edges_high, parts = [], [], []
@@ -310,16 +342,17 @@
 
 VM = pl.BlockSpec(memory_space=pltpu.VMEM)
 SM = pl.BlockSpec(memory_space=pltpu.SMEM)
-
-
-def call(kernel, outs, args, specs=None, scratch=()):
+HBM = pl.BlockSpec(memory_space=pltpu.HBM)
+
+
+def call(kernel, outs, args, specs=None, scratch=(), limit=32):
     return pl.pallas_call(
         kernel,
         out_shape=[jax.ShapeDtypeStruct(shape, kind) for shape, kind in outs],
         in_specs=specs or [SM] + [VM] * (len(args) - 1),
         out_specs=[VM] * len(outs),
         scratch_shapes=[pltpu.VMEM(s, F32) if isinstance(s, tuple) else s for s in scratch],
-        compiler_params=pltpu.CompilerParams(vmem_limit_bytes=32 * 2**20),
+        compiler_params=pltpu.CompilerParams(vmem_limit_bytes=limit * 2**20),
         name=kernel.__name__,
     )(*args)
 
@@ -327,8 +360,7 @@
 def shards(data, blocks, block_cols, block_rows, block_counts, reg_weight):
     pos = jnp.stack([lax.axis_index("ray"), lax.axis_index("tile")]).astype(jnp.int32)
     weight = reg_weight.reshape(CELLS, LANES)
-    message = ((RAY, MSG, LANES), F32)
-    half_message = ((RAY, MSG, LANES), BF16)
+    message = ((RAY, MSG, LANES), BF16)
     tile_message = ((TILE, TMSG, LANES), BF16)
     scalar = ((1, LANES), F32)
     cells = ((CELLS, LANES), F32)
@@ -338,23 +370,30 @@
     slabs = [(XS + 2, CY, LANES), (TILE, 8, LANES)]
     own = jnp.concatenate([data.reshape(KOWN, LANES), weight], axis=0)
     start = lax.all_to_all(jnp.broadcast_to(own, (TILE,) + own.shape), "tile", 0, 0)
-    p_hot, p_wide, r_hot, note = call(
+    p_hot, p_wide, r_hot, r_turned, note = call(
         kernel_index,
         [
             ((RAY * CAP, SLOTS), BF16),
-            ((RAY * MSG, SLOTS), BF16),
+            ((SLOTS, RAY * MSG), BF16),
             ((KB, SLOTS), BF16),
+            ((SLOTS, KB), BF16),
             ((RAY * CAP, LANES), F32),
         ],
         (block_cols[0], block_rows[0], block_counts),
         [VM] * 3,
     )
-    values = blocks[0, 0]
-    (send,) = call(kernel_start, [message], (pos, start, note, values, p_hot, r_hot))
+    send, values = call(
+        kernel_start,
+        [message, ((SLOTS, LANES, LANES), BF16)],
+        (pos, start, note, blocks[0, 0], p_hot, r_turned),
+        [SM, VM, VM, HBM, VM, VM],
+        [pltpu.SemaphoreType.DMA((CHUNKS,))],
+        48,
+    )
     recv = lax.all_to_all(send, "ray", 0, 0)
     send, v0_raw, q_hot, beta0 = call(
         kernel_first_v,
-        [half_message, cells, ((RAY * CAP, CELLS), BF16), scalar],
+        [message, cells, ((RAY * CAP, CELLS), BF16), scalar],
         (pos, recv),
         scratch=[edges],
     )
@@ -366,13 +405,13 @@
     send, raw1, raw2, alpha0, nq = call(
         kernel_back,
         [message, rays, slab, scalar, cells],
-        (pos, recv, v0_raw, start, beta0, values, p_hot, r_hot),
+        (pos, recv, v0_raw, start, beta0, values, p_hot, r_turned),
         scratch=[edges] + slabs + slabs[:1],
     )
     recv = lax.all_to_all(send, "ray", 0, 0)
     send, v1_raw, beta1 = call(
         kernel_next_v,
-        [half_message, cells, scalar],
+        [message, cells, scalar],
         (pos, recv, q_hot, v0_raw, alpha0, nq),
         scratch=[edges],
     )

time: 124 us -> 121 us (0.976)
  blocking collectives: 91.9 us -> 89.5 us
  local copies, waits for them, and re-layouts: 4.17 us -> 1.97 us
  Pallas kernels: 10.9 us -> 12.3 us
    all_to_all x5, blocking collectives: 64 us -> 61.6 us  [shards(): recv = lax.all_to_all(send, 'ray', 0, 0)]
    unnamed x8 -> x4, local copies, waits for them, and re-layouts: 3.5 us -> 1.31 us
    pallas_call x9, Pallas kernels: 10.9 us -> 12.3 us  [call(): pl.pallas_call(kernel, out_shape=[jax.ShapeDtypeStruct(shape, kind) for s...]
where the time goes in v3:
time: 121 us
  blocking collectives  89.5 us (74%)
  Pallas kernels  12.3 us (10%)
  starting transfers between devices  9.01 us (7%)
  waiting for transfers between devices  5.76 us (5%)
  local copies, waits for them, and re-layouts  1.97 us (2%)
  between operations  1.35 us (1%)
    all_to_all x5, blocking collectives, shards(): recv = lax.all_to_all(send, 'ray', 0, 0)  61.6 us
    all_to_all x2, blocking collectives, shards(): recv = lax.all_to_all(send, 'tile', 0, 0)  27.9 us
    pallas_call x9, Pallas kernels, call(): pl.pallas_call(kernel, out_shape=[jax.ShapeDtypeStruct(shape, kind) for s...  12.3 us
    all_to_all x1, starting transfers between devices, shards(): lax.all_to_all(jnp.broadcast_to(own, (TILE,) + own.shape), 'tile', 0, 0)  9.01 us
    all_to_all x1, waiting for transfers between devices, shards(): lax.all_to_all(jnp.broadcast_to(own, (TILE,) + own.shape), 'tile', 0, 0)  5.76 us
  transfers between devices with their start and end apart: 1, of which 1 were waited for; matrix products, arithmetic and copies ran while one was open for 0% of the time, Pallas kernels for 0%

profile of v3, /device:TPU:1, one launch (start us, length us, event | category | flops | bytes accessed | tf_op | source)
XLA Modules:
  0.0 120.7 jit_solution(8699635038244038817)
XLA Ops:
  0.6 0.7 pad_maximum_fusion
  1.4 0.7 broadcast_in_dim.3
  2.0 9.0 %all-to-all-start = ((f32[8,40,128]{2,1,0:T(8,128)}), f32[8,40,128]{2,1,0:T(8,128)S(1)}, u32[]{:S(2)}, u32[]{:S(2)}) async-start(f32[8,40,128]{2,1,0:T(8,128)} %broadcast_in_dim.3), calls=%async_computation | async-start | bytes 327680 | tf_op jit(solution)/shard_map/all_to_all | solution.py:372
  11.7 0.0 copy-start
  11.7 0.6 copy-done
  12.3 0.0 copy-start.1
  12.3 0.7 copy-done.1
  13.0 0.3 kernel_index.1
  13.3 0.1 pad_add_fusion.pos_ref
  13.4 5.8 %all-to-all-done.start = f32[8,40,128]{2,1,0:T(8,128)S(1)} async-done(((f32[8,40,128]{2,1,0:T(8,128)}), f32[8,40,128]{2,1,0:T(8,128)S(1)}, u32[]{:S(2)}, u32[]{:S(2)}) %all-to-all-start) | async-done | bytes 163872 | tf_op jit(solution)/shard_map/all_to_all | solution.py:372
  19.2 3.2 %kernel_start.1 = (bf16[32,16,128]{2,1,0:T(8,128)(2,1)S(1)}, bf16[128,128,128]{2,1,0:T(8,128)(2,1)S(1)}) custom-call(s32[2]{0:T(128)S(1)} %pad_add_fusion.pos_ref, f32[8,40,128]{2,1,0:T(8,128)S(1)} %all-to-all-done.start, f32[256,128]{1,0:T(8,128)S(1)} %get-tuple-element.26.note, bf16[128,128,128]{2,1,0:T(8,128)(2,1)} %bitcast.11, ...), custom_call_target="tpu_custom_call" | custom-call | tf_op jit(solution)/shard_map/kernel_start/pallas_call | solution.py:349
  22.3 17.2 %all_to_all.40.recv = bf16[32,16,128]{2,1,0:T(8,128)(2,1)S(1)} all-to-all(bf16[32,16,128]{2,1,0:T(8,128)(2,1)S(1)} %get-tuple-element.29), channel_id=1, replica_groups=mesh['ray'=32,'tile'=8] {'ray'}, dimensions={0} | all-to-all | bytes 262144 | tf_op jit(solution)/shard_map/all_to_all | solution.py:393
  39.5 0.9 kernel_first_v.1
  40.4 11.3 %all_to_all.41.recv = bf16[32,16,128]{2,1,0:T(8,128)(2,1)S(1)} all-to-all(bf16[32,16,128]{2,1,0:T(8,128)(2,1)S(1)} %get-tuple-element.30), channel_id=1, replica_groups=mesh['ray'=32,'tile'=8] {'ray'}, dimensions={0} | all-to-all | bytes 262144 | tf_op jit(solution)/shard_map/all_to_all | solution.py:400
  51.7 2.1 %kernel_forward.2 = bf16[8,112,128]{2,1,0:T(8,128)(2,1)S(1)} custom-call(s32[2]{0:T(128)S(1)} %pad_add_fusion.pos_ref, bf16[32,16,128]{2,1,0:T(8,128)(2,1)S(1)} %all_to_all.41.recv, bf16[128,512]{1,0:T(8,128)(2,1)S(1)} %get-tuple-element.31.p_wide, bf16[64,128]{1,0:T(8,128)(2,1)S(1)} %get-tuple-element.32.r_hot, ...), custom_call_target="tpu_custom_call" | custom-call | tf_op jit(solution)/shard_map/kernel_forward/pallas_call | solution.py:349
  53.7 13.9 %all_to_all.42.recv = bf16[8,112,128]{2,1,0:T(8,128)(2,1)S(1)} all-to-all(bf16[8,112,128]{2,1,0:T(8,128)(2,1)S(1)} %kernel_forward.2), channel_id=1, replica_groups=mesh['ray'=32,'tile'=8] {'tile'}, dimensions={0} | all-to-all | bytes 458752 | tf_op jit(solution)/shard_map/all_to_all | solution.py:404
  67.7 1.5 %kernel_back.1 = (bf16[32,16,128]{2,1,0:T(8,128)(2,1)S(1)}, f32[64,128]{1,0:T(8,128)S(1)}, f32[32,8,128]{2,1,0:T(8,128)S(1)}, f32[1,128]{1,0:T(1,128)S(1)}, f32[32,128]{1,0:T(8,128)S(1)}) custom-call(s32[2]{0:T(128)S(1)} %pad_add_fusion.pos_ref, bf16[8,112,128]{2,1,0:T(8,128)(2,1)S(1)} %all_to_all.42.recv, f32[32,128]{1,0:T(8,128)S(1)} %get-tuple-element.34.v_raw.v0_raw, ...), custom_call_target="tpu_custom_call" | custom-call | tf_op jit(solution)/shard_map/kernel_back/pallas_call | solution.py:349
  69.2 11.3 %all_to_all.43.recv = bf16[32,16,128]{2,1,0:T(8,128)(2,1)S(1)} all-to-all(bf16[32,16,128]{2,1,0:T(8,128)(2,1)S(1)} %get-tuple-element.36), channel_id=1, replica_groups=mesh['ray'=32,'tile'=8] {'ray'}, dimensions={0} | all-to-all | bytes 262144 | tf_op jit(solution)/shard_map/all_to_all | solution.py:411
  80.5 0.9 kernel_next_v.1
  81.4 11.3 %all_to_all.44.recv = bf16[32,16,128]{2,1,0:T(8,128)(2,1)S(1)} all-to-all(bf16[32,16,128]{2,1,0:T(8,128)(2,1)S(1)} %get-tuple-element.40), channel_id=1, replica_groups=mesh['ray'=32,'tile'=8] {'ray'}, dimensions={0} | all-to-all | bytes 262144 | tf_op jit(solution)/shard_map/all_to_all | solution.py:418
  92.7 2.1 %kernel_forward.3 = bf16[8,112,128]{2,1,0:T(8,128)(2,1)S(1)} custom-call(s32[2]{0:T(128)S(1)} %pad_add_fusion.pos_ref, bf16[32,16,128]{2,1,0:T(8,128)(2,1)S(1)} %all_to_all.44.recv, bf16[128,512]{1,0:T(8,128)(2,1)S(1)} %get-tuple-element.31.p_wide, bf16[64,128]{1,0:T(8,128)(2,1)S(1)} %get-tuple-element.32.r_hot, ...), custom_call_target="tpu_custom_call" | custom-call | tf_op jit(solution)/shard_map/kernel_forward/pallas_call | solution.py:349
  94.7 13.9 %all_to_all.45.recv = bf16[8,112,128]{2,1,0:T(8,128)(2,1)S(1)} all-to-all(bf16[8,112,128]{2,1,0:T(8,128)(2,1)S(1)} %kernel_forward.3), channel_id=1, replica_groups=mesh['ray'=32,'tile'=8] {'tile'}, dimensions={0} | all-to-all | bytes 458752 | tf_op jit(solution)/shard_map/all_to_all | solution.py:422
  108.7 0.8 kernel_last_norm.1
  109.5 10.6 %all_to_all.46.recv = f32[32,1,128]{2,1,0:T(1,128)S(1)} all-to-all(f32[32,1,128]{2,1,0:T(1,128)S(1)} %get-tuple-element.45), channel_id=1, replica_groups=mesh['ray'=32,'tile'=8] {'ray'}, dimensions={0} | all-to-all | bytes 32768 | tf_op jit(solution)/shard_map/all_to_all | solution.py:429
  120.0 0.7 kernel_end.1
Async XLA Ops:
  2.0 17.2 %all-to-all-start = ((f32[8,40,128]{2,1,0:T(8,128)}), f32[8,40,128]{2,1,0:T(8,128)S(1)}, u32[]{:S(2)}, u32[]{:S(2)}) async-start(f32[8,40,128]{2,1,0:T(8,128)} %broadcast_in_dim.3), calls=%async_computation | async-start | bytes 327680 | tf_op jit(solution)/shard_map/all_to_all | solution.py:372
  11.7 0.7 copy-start
  12.3 0.7 copy-start.1

commit v4 on v3

--- a/solution.py
+++ b/solution.py
@@ -18,7 +18,8 @@
 MSG = 2 * CAP
 TMSG = KB + CELLS + 16
 SMSG = KOWN + CELLS
-CHUNKS = 4
+HALF = SLOTS // 2
+CHUNKS = 2
 XS = TILE * CX
 eps = 1e-06
 
@@ -70,24 +71,40 @@
     return below + above
 
 
-def products_t(picked, blocks, first):
+def eight(pair, at):
+    first, second = pair
+    return first[at : at + 8] if at < HALF else second[at - HALF : at - HALF + 8]
+
+
+def bring(blocks, start, held, sems):
+    per = HALF // CHUNKS
+    copies = [
+        pltpu.make_async_copy(blocks.at[pl.ds(start + c * per, per)], held.at[pl.ds(c * per, per)], sems.at[c])
+        for c in range(CHUNKS)
+    ]
+    for copy in copies:
+        copy.start()
+    return copies
+
+
+def products_t(picked, pair, start, stop):
     row = iota((8, LANES), 0)
     out = []
-    for q in range(picked.shape[0] // 8):
-        p = picked[8 * q : 8 * q + 8, :]
+    for at in range(start, stop, 8):
+        p = picked[at : at + 8, :]
         lhs = jnp.concatenate([jnp.where(row == i, p, 0.0) for i in range(8)], axis=1)
-        at = first + 8 * q
-        out.append(dot(lhs.astype(BF16), blocks[at : at + 8].reshape(8 * LANES, LANES), 1, 0))
-    return jnp.concatenate(out, axis=0)
-
-
-def products(x, blocks, r_hot):
+        out.append(dot(lhs.astype(BF16), eight(pair, at).reshape(8 * LANES, LANES), 1, 0))
+    return out
+
+
+def products(x, pair, r_hot):
     row = iota((8, LANES), 0)
     out = []
     for q in range(SLOTS // 8):
         p = x[8 * q : 8 * q + 8, :]
         lhs = jnp.concatenate([jnp.where(row == i, p, 0.0) for i in range(8)], axis=1)
-        rhs = jnp.concatenate([blocks[8 * q + i] for i in range(8)], axis=1)
+        some = eight(pair, 8 * q)
+        rhs = jnp.concatenate([some[i] for i in range(8)], axis=1)
         out.append(dot(lhs.astype(BF16), rhs, 1, 1))
     return onehot_dot(r_hot, jnp.concatenate(out, axis=0), 1, 0)
 
@@ -104,7 +121,8 @@
     return scratch[0], scratch[1]
 
 
-def kernel_index(cols, rows, count, p_out, p_wide_out, r_out, r_turned_out, note_out):
+def kernel_index(cols, rows, count, blocks, p_out, p_wide_out, r_out, r_turned_out, note_out, first_out, sems):
+    copies = bring(blocks, 0, first_out, sems)
     col = cols[...]
     live = iota((1, SLOTS), 1) < count[...]
     slab = RAY * CY
@@ -123,6 +141,8 @@
     r_turned_out[...] = r_f.T.astype(BF16)
     ids = jnp.sum(p_f * (local + 1).astype(F32), axis=1, keepdims=True) - 1.0
     note_out[...] = jnp.broadcast_to(ids, (RAY * CAP, LANES))
+    for copy in copies:
+        copy.wait()
 
 
 def send_contributions(send, p_hot, contrib, notes):
@@ -137,20 +157,16 @@
     return contrib, [x[CAP:MSG] for x in both]
 
 
-def kernel_start(pos_ref, start, note, blocks, p_hot, r_turned, send, held, sems):
-    per = SLOTS // CHUNKS
-    copies = [
-        pltpu.make_async_copy(blocks.at[pl.ds(c * per, per)], held.at[pl.ds(c * per, per)], sems.at[c])
-        for c in range(CHUNKS)
-    ]
-    for copy in copies:
-        copy.start()
+def kernel_start(pos_ref, start, note, blocks, first, p_hot, r_turned, send, second_out, sems):
+    copies = bring(blocks, HALF, second_out, sems)
     data = start[:, 0:KOWN, :].reshape(KB, LANES)
     picked = dot(r_turned[...], data.astype(BF16), 1, 0)
-    contrib = []
+    pair = (first, second_out)
+    contrib = products_t(picked, pair, 0, HALF)
+    per = HALF // CHUNKS
     for c, copy in enumerate(copies):
         copy.wait()
-        contrib.append(products_t(picked[c * per : (c + 1) * per], held, c * per))
+        contrib += products_t(picked, pair, HALF + c * per, HALF + (c + 1) * per)
     contrib = jnp.concatenate(contrib, axis=0)
     quarter = iota((CAP, LANES), 1) // CELLS
     high, mid, low = terms(total(data * data))
@@ -188,10 +204,10 @@
     send_columns(send, q_hot, v_raw, scratch, low, high, total(v_raw * v_raw), pos_ref[0])
 
 
-def kernel_forward(pos_ref, recv, p_wide, r_hot, blocks, v_raw, send, scratch):
+def kernel_forward(pos_ref, recv, p_wide, r_hot, first, second, v_raw, send, scratch):
     ray = pos_ref[0]
     x = dot(p_wide[...], recv[...].reshape(RAY * MSG, LANES), 1, 0)
-    part = products(x, blocks, r_hot[...]).astype(BF16)
+    part = products(x, (first, second), r_hot[...]).astype(BF16)
     norm = jnp.zeros((MSG, LANES), F32)
     for d in range(RAY):
         norm = norm + recv[d].astype(F32)
@@ -246,7 +262,7 @@
 
 
 def kernel_back(
-    pos_ref, recv, v_raw, start, beta0, blocks, p_hot, r_turned,
+    pos_ref, recv, v_raw, start, beta0, first, second, p_hot, r_turned,
     send, raw1_out, raw2_out, alpha_out, nq_out,
     scratch, slab, edges, field,
 ):
@@ -264,7 +280,8 @@
         raw2_out[i] = raw2
         squares = squares + raw2 * raw2
         field[i + 1] = weight * raw2
-    contrib = products_t(dot(r_turned[...], raw1.astype(BF16), 1, 0), blocks, 0)
+    picked = dot(r_turned[...], raw1.astype(BF16), 1, 0)
+    contrib = jnp.concatenate(products_t(picked, (first, second), 0, SLOTS), axis=0)
     low, high = [], []
     for x in range(CX):
         at = tile * CX + x + 1
@@ -370,7 +387,8 @@
     slabs = [(XS + 2, CY, LANES), (TILE, 8, LANES)]
     own = jnp.concatenate([data.reshape(KOWN, LANES), weight], axis=0)
     start = lax.all_to_all(jnp.broadcast_to(own, (TILE,) + own.shape), "tile", 0, 0)
-    p_hot, p_wide, r_hot, r_turned, note = call(
+    half = ((HALF, LANES, LANES), BF16)
+    p_hot, p_wide, r_hot, r_turned, note, first = call(
         kernel_index,
         [
             ((RAY * CAP, SLOTS), BF16),
@@ -378,15 +396,18 @@
             ((KB, SLOTS), BF16),
             ((SLOTS, KB), BF16),
             ((RAY * CAP, LANES), F32),
+            half,
         ],
-        (block_cols[0], block_rows[0], block_counts),
-        [VM] * 3,
-    )
-    send, values = call(
+        (block_cols[0], block_rows[0], block_counts, blocks[0, 0]),
+        [VM] * 3 + [HBM],
+        [pltpu.SemaphoreType.DMA((CHUNKS,))],
+        50,
+    )
+    send, second = call(
         kernel_start,
-        [message, ((SLOTS, LANES, LANES), BF16)],
-        (pos, start, note, blocks[0, 0], p_hot, r_turned),
-        [SM, VM, VM, HBM, VM, VM],
+        [message, half],
+        (pos, start, note, blocks[0, 0], first, p_hot, r_turned),
+        [SM, VM, VM, HBM, VM, VM, VM],
         [pltpu.SemaphoreType.DMA((CHUNKS,))],
         48,
     )
@@ -399,13 +420,13 @@
     )
     recv = lax.all_to_all(send, "ray", 0, 0)
     (send,) = call(
-        kernel_forward, [tile_message], (pos, recv, p_wide, r_hot, values, v0_raw), scratch=[(16, LANES)]
+        kernel_forward, [tile_message], (pos, recv, p_wide, r_hot, first, second, v0_raw), scratch=[(16, LANES)]
     )
     recv = lax.all_to_all(send, "tile", 0, 0)
     send, raw1, raw2, alpha0, nq = call(
         kernel_back,
         [message, rays, slab, scalar, cells],
-        (pos, recv, v0_raw, start, beta0, values, p_hot, r_turned),
+        (pos, recv, v0_raw, start, beta0, first, second, p_hot, r_turned),
         scratch=[edges] + slabs + slabs[:1],
     )
     recv = lax.all_to_all(send, "ray", 0, 0)
@@ -417,7 +438,7 @@
     )
     recv = lax.all_to_all(send, "ray", 0, 0)
     (send,) = call(
-        kernel_forward, [tile_message], (pos, recv, p_wide, r_hot, values, v1_raw), scratch=[(16, LANES)]
+        kernel_forward, [tile_message], (pos, recv, p_wide, r_hot, first, second, v1_raw), scratch=[(16, LANES)]
     )
     recv = lax.all_to_all(send, "tile", 0, 0)
     send, raw1_own, alpha1 = call(

time: 121 us -> 121 us (level)
  waiting for transfers between devices: 5.76 us -> 4.49 us
    all_to_all x1, waiting for transfers between devices: 5.76 us -> 4.49 us  [shards(): lax.all_to_all(jnp.broadcast_to(own, (TILE,) + own.shape), 'tile', 0, 0)]
  transfers between devices with their start and end apart: 1 -> 1, of which waited for: 1 -> 1; matrix products, arithmetic and copies ran while one was open for 0% -> 0% of each run, Pallas kernels for 0% -> 1%
where the time goes in v4:
time: 121 us; the launch traced here: 120 us
  blocking collectives  89.5 us (74%)
  Pallas kernels  12.9 us (11%)
  starting transfers between devices  9.01 us (7%)
  waiting for transfers between devices  4.49 us (4%)
  local copies, waits for them, and re-layouts  1.97 us (2%)
  between operations  1.36 us (1%)
    all_to_all x5, blocking collectives, shards(): recv = lax.all_to_all(send, 'ray', 0, 0)  61.6 us
    all_to_all x2, blocking collectives, shards(): recv = lax.all_to_all(send, 'tile', 0, 0)  27.9 us
    pallas_call x9, Pallas kernels, call(): pl.pallas_call(kernel, out_shape=[jax.ShapeDtypeStruct(shape, kind) for s...  12.9 us
    all_to_all x1, starting transfers between devices, shards(): lax.all_to_all(jnp.broadcast_to(own, (TILE,) + own.shape), 'tile', 0, 0)  9.01 us
    all_to_all x1, waiting for transfers between devices, shards(): lax.all_to_all(jnp.broadcast_to(own, (TILE,) + own.shape), 'tile', 0, 0)  4.49 us
  transfers between devices with their start and end apart: 1, of which 1 were waited for; matrix products, arithmetic and copies ran while one was open for 0% of the time, Pallas kernels for 1%

profile of v4, /device:TPU:1, one launch (start us, length us, event | category | flops | bytes accessed | tf_op | source)
XLA Modules:
  0.0 120.1 jit_solution(12359774034231493180)
XLA Ops:
  0.6 0.7 pad_maximum_fusion
  1.4 0.7 broadcast_in_dim.3
  2.0 9.0 %all-to-all-start = ((f32[8,40,128]{2,1,0:T(8,128)}), f32[8,40,128]{2,1,0:T(8,128)S(1)}, u32[]{:S(2)}, u32[]{:S(2)}) async-start(f32[8,40,128]{2,1,0:T(8,128)} %broadcast_in_dim.3), calls=%async_computation | async-start | bytes 327680 | tf_op jit(solution)/shard_map/all_to_all | solution.py:389
  11.7 0.0 copy-start
  11.7 0.6 copy-done
  12.3 0.0 copy-start.1
  12.3 0.7 copy-done.1
  13.0 1.6 %kernel_index.1 = (bf16[256,128]{1,0:T(8,128)(2,1)S(1)}, bf16[128,512]{1,0:T(8,128)(2,1)S(1)}, bf16[64,128]{1,0:T(8,128)(2,1)S(1)}, bf16[128,64]{1,0:T(8,128)(2,...) custom-call(s32[1,128]{1,0:T(1,128)S(1)} %bitcast.9, s32[1,128]{1,0:T(1,128)S(1)} %bitcast.10, ...), custom_call_target="tpu_custom_call" | custom-call | tf_op jit(solution)/shard_map/kernel_index/pallas_call | solution.py:366
  14.6 0.1 pad_add_fusion.pos_ref
  14.7 4.5 %all-to-all-done.start = f32[8,40,128]{2,1,0:T(8,128)S(1)} async-done(((f32[8,40,128]{2,1,0:T(8,128)}), f32[8,40,128]{2,1,0:T(8,128)S(1)}, u32[]{:S(2)}, u32[]{:S(2)}) %all-to-all-start) | async-done | bytes 163872 | tf_op jit(solution)/shard_map/all_to_all | solution.py:389
  19.2 2.5 %kernel_start.1 = (bf16[32,16,128]{2,1,0:T(8,128)(2,1)S(1)}, bf16[64,128,128]{2,1,0:T(8,128)(2,1)S(1)}) custom-call(s32[2]{0:T(128)S(1)} %pad_add_fusion.pos_ref, f32[8,40,128]{2,1,0:T(8,128)S(1)} %all-to-all-done.start, f32[256,128]{1,0:T(8,128)S(1)} %get-tuple-element.27.note, bf16[128,128,128]{2,1,0:T(8,128)(2,1)} %bitcast.12, ...), custom_call_target="tpu_custom_call" | custom-call | tf_op jit(solution)/shard_map/kernel_start/pallas_call | solution.py:366
  21.7 17.2 %all_to_all.40.recv = bf16[32,16,128]{2,1,0:T(8,128)(2,1)S(1)} all-to-all(bf16[32,16,128]{2,1,0:T(8,128)(2,1)S(1)} %get-tuple-element.31), channel_id=1, replica_groups=mesh['ray'=32,'tile'=8] {'ray'}, dimensions={0} | all-to-all | bytes 262144 | tf_op jit(solution)/shard_map/all_to_all | solution.py:414
  38.9 0.9 kernel_first_v.1
  39.7 11.3 %all_to_all.41.recv = bf16[32,16,128]{2,1,0:T(8,128)(2,1)S(1)} all-to-all(bf16[32,16,128]{2,1,0:T(8,128)(2,1)S(1)} %get-tuple-element.32), channel_id=1, replica_groups=mesh['ray'=32,'tile'=8] {'ray'}, dimensions={0} | all-to-all | bytes 262144 | tf_op jit(solution)/shard_map/all_to_all | solution.py:421
  51.0 2.1 %kernel_forward.2 = bf16[8,112,128]{2,1,0:T(8,128)(2,1)S(1)} custom-call(s32[2]{0:T(128)S(1)} %pad_add_fusion.pos_ref, bf16[32,16,128]{2,1,0:T(8,128)(2,1)S(1)} %all_to_all.41.recv, bf16[128,512]{1,0:T(8,128)(2,1)S(1)} %get-tuple-element.33.p_wide, bf16[64,128]{1,0:T(8,128)(2,1)S(1)} %get-tuple-element.34.r_hot, ...), custom_call_target="tpu_custom_call" | custom-call | tf_op jit(solution)/shard_map/kernel_forward/pallas_call | solution.py:366
  53.1 13.9 %all_to_all.42.recv = bf16[8,112,128]{2,1,0:T(8,128)(2,1)S(1)} all-to-all(bf16[8,112,128]{2,1,0:T(8,128)(2,1)S(1)} %kernel_forward.2), channel_id=1, replica_groups=mesh['ray'=32,'tile'=8] {'tile'}, dimensions={0} | all-to-all | bytes 458752 | tf_op jit(solution)/shard_map/all_to_all | solution.py:425
  67.0 1.5 %kernel_back.1 = (bf16[32,16,128]{2,1,0:T(8,128)(2,1)S(1)}, f32[64,128]{1,0:T(8,128)S(1)}, f32[32,8,128]{2,1,0:T(8,128)S(1)}, f32[1,128]{1,0:T(1,128)S(1)}, f32[32,128]{1,0:T(8,128)S(1)}) custom-call(s32[2]{0:T(128)S(1)} %pad_add_fusion.pos_ref, bf16[8,112,128]{2,1,0:T(8,128)(2,1)S(1)} %all_to_all.42.recv, f32[32,128]{1,0:T(8,128)S(1)} %get-tuple-element.36.v_raw.v0_raw, ...), custom_call_target="tpu_custom_call" | custom-call | tf_op jit(solution)/shard_map/kernel_back/pallas_call | solution.py:366
  68.5 11.3 %all_to_all.43.recv = bf16[32,16,128]{2,1,0:T(8,128)(2,1)S(1)} all-to-all(bf16[32,16,128]{2,1,0:T(8,128)(2,1)S(1)} %get-tuple-element.38), channel_id=1, replica_groups=mesh['ray'=32,'tile'=8] {'ray'}, dimensions={0} | all-to-all | bytes 262144 | tf_op jit(solution)/shard_map/all_to_all | solution.py:432
  79.9 0.9 kernel_next_v.1
  80.7 11.3 %all_to_all.44.recv = bf16[32,16,128]{2,1,0:T(8,128)(2,1)S(1)} all-to-all(bf16[32,16,128]{2,1,0:T(8,128)(2,1)S(1)} %get-tuple-element.42), channel_id=1, replica_groups=mesh['ray'=32,'tile'=8] {'ray'}, dimensions={0} | all-to-all | bytes 262144 | tf_op jit(solution)/shard_map/all_to_all | solution.py:439
  92.0 2.1 %kernel_forward.3 = bf16[8,112,128]{2,1,0:T(8,128)(2,1)S(1)} custom-call(s32[2]{0:T(128)S(1)} %pad_add_fusion.pos_ref, bf16[32,16,128]{2,1,0:T(8,128)(2,1)S(1)} %all_to_all.44.recv, bf16[128,512]{1,0:T(8,128)(2,1)S(1)} %get-tuple-element.33.p_wide, bf16[64,128]{1,0:T(8,128)(2,1)S(1)} %get-tuple-element.34.r_hot, ...), custom_call_target="tpu_custom_call" | custom-call | tf_op jit(solution)/shard_map/kernel_forward/pallas_call | solution.py:366
  94.1 13.9 %all_to_all.45.recv = bf16[8,112,128]{2,1,0:T(8,128)(2,1)S(1)} all-to-all(bf16[8,112,128]{2,1,0:T(8,128)(2,1)S(1)} %kernel_forward.3), channel_id=1, replica_groups=mesh['ray'=32,'tile'=8] {'tile'}, dimensions={0} | all-to-all | bytes 458752 | tf_op jit(solution)/shard_map/all_to_all | solution.py:443
  108.0 0.8 kernel_last_norm.1
  108.8 10.6 %all_to_all.46.recv = f32[32,1,128]{2,1,0:T(1,128)S(1)} all-to-all(f32[32,1,128]{2,1,0:T(1,128)S(1)} %get-tuple-element.47), channel_id=1, replica_groups=mesh['ray'=32,'tile'=8] {'ray'}, dimensions={0} | all-to-all | bytes 32768 | tf_op jit(solution)/shard_map/all_to_all | solution.py:450
  119.4 0.7 kernel_end.1
Async XLA Ops:
  2.0 17.2 %all-to-all-start = ((f32[8,40,128]{2,1,0:T(8,128)}), f32[8,40,128]{2,1,0:T(8,128)S(1)}, u32[]{:S(2)}, u32[]{:S(2)}) async-start(f32[8,40,128]{2,1,0:T(8,128)} %broadcast_in_dim.3), calls=%async_computation | async-start | bytes 327680 | tf_op jit(solution)/shard_map/all_to_all | solution.py:389
  11.7 0.7 copy-start
  12.3 0.7 copy-start.1

commit v5 on v4

--- a/solution.py
+++ b/solution.py
@@ -1,3 +1,5 @@
+import functools
+
 import jax
 import jax.numpy as jnp
 from jax import lax
@@ -97,15 +99,18 @@
     return out
 
 
-def products(x, pair, r_hot):
+def products(parts, pair, r_hot):
     row = iota((8, LANES), 0)
     out = []
     for q in range(SLOTS // 8):
-        p = x[8 * q : 8 * q + 8, :]
-        lhs = jnp.concatenate([jnp.where(row == i, p, 0.0) for i in range(8)], axis=1)
+        lhs = [
+            jnp.concatenate([jnp.where(row == i, x[8 * q : 8 * q + 8, :], 0.0) for i in range(8)], axis=1)
+            for x in parts
+        ]
         some = eight(pair, 8 * q)
         rhs = jnp.concatenate([some[i] for i in range(8)], axis=1)
-        out.append(dot(lhs.astype(BF16), rhs, 1, 1))
+        both = dot(jnp.concatenate(lhs, axis=0).astype(BF16), rhs, 1, 1)
+        out.append(both[0:8] + both[8:16] if len(parts) == 2 else both)
     return onehot_dot(r_hot, jnp.concatenate(out, axis=0), 1, 0)
 
 
@@ -178,11 +183,11 @@
 
 
 def send_columns(send, q_hot, v_raw, scratch, low, high, scalar, ray):
-    columns = dot(q_hot, v_raw.astype(BF16), 1, 0)
+    columns = onehot_dot(q_hot, v_raw, 1, 0)
     low, high = edge_tiles(scratch, low, high, scalar)
     for d in range(RAY):
         edge = jnp.where(d > ray, high, low)
-        send[d] = jnp.concatenate([columns[CAP * d : CAP * d + CAP], edge], axis=0).astype(BF16)
+        send[d] = jnp.concatenate([columns[CAP * d : CAP * d + CAP], edge], axis=0).astype(send.dtype)
 
 
 def kernel_first_v(pos_ref, recv, send, v_out, q_out, beta_out, scratch):
@@ -204,10 +209,15 @@
     send_columns(send, q_hot, v_raw, scratch, low, high, total(v_raw * v_raw), pos_ref[0])
 
 
-def kernel_forward(pos_ref, recv, p_wide, r_hot, first, second, v_raw, send, scratch):
+def kernel_forward(pos_ref, recv, p_wide, r_hot, first, second, v_raw, send, scratch, *, last):
     ray = pos_ref[0]
-    x = dot(p_wide[...], recv[...].reshape(RAY * MSG, LANES), 1, 0)
-    part = products(x, (first, second), r_hot[...]).astype(BF16)
+    asked = recv[...].reshape(RAY * MSG, LANES)
+    parts = [asked.astype(BF16)]
+    if last:
+        parts.append((asked - parts[0].astype(F32)).astype(BF16))
+    full = products([dot(p_wide[...], x, 1, 0) for x in parts], (first, second), r_hot[...])
+    part = full.astype(BF16)
+    rest = full - part.astype(F32)
     norm = jnp.zeros((MSG, LANES), F32)
     for d in range(RAY):
         norm = norm + recv[d].astype(F32)
@@ -226,6 +236,9 @@
         send[t, 0:KB, :] = part
         send[t, KB : KB + CELLS, :] = mine
         send[t, KB + CELLS : TMSG, :] = edge
+        if last:
+            own = rest[KOWN * t : KOWN * t + KOWN]
+            send[t, TMSG : TMSG + 16, :] = jnp.concatenate([own, jnp.zeros_like(own)], axis=0).astype(BF16)
 
 
 def gathered(recv, v_raw, tile, slab, edges):
@@ -329,7 +342,10 @@
     alpha_out[...] = alpha
     raw1 = kv / alpha - alpha * (raw1_ref[...] / beta1[...])
     scratch[...] = raw1.reshape(TILE, KOWN, LANES)
-    raw1_out[...] = scratch[tile]
+    rest = recv[0, TMSG : TMSG + 16, :].astype(F32)[0:KOWN]
+    for t in range(1, TILE):
+        rest = rest + recv[t, TMSG : TMSG + 16, :].astype(F32)[0:KOWN]
+    raw1_out[...] = scratch[tile] + rest / alpha
     squares = jnp.zeros((CY, LANES), F32)
     for i in range(XS):
         raw2 = cell_weight(start, i) * (slab_laplace(slab, edges, i) / alpha) - alpha * (raw2_ref[i] / beta1[...])
@@ -370,7 +386,7 @@
         out_specs=[VM] * len(outs),
         scratch_shapes=[pltpu.VMEM(s, F32) if isinstance(s, tuple) else s for s in scratch],
         compiler_params=pltpu.CompilerParams(vmem_limit_bytes=limit * 2**20),
-        name=kernel.__name__,
+        name=getattr(kernel, "func", kernel).__name__,
     )(*args)
 
 
@@ -420,7 +436,8 @@
     )
     recv = lax.all_to_all(send, "ray", 0, 0)
     (send,) = call(
-        kernel_forward, [tile_message], (pos, recv, p_wide, r_hot, first, second, v0_raw), scratch=[(16, LANES)]
+        functools.partial(kernel_forward, last=False), [((TILE, TMSG, LANES), BF16)],
+        (pos, recv, p_wide, r_hot, first, second, v0_raw), scratch=[(16, LANES)],
     )
     recv = lax.all_to_all(send, "tile", 0, 0)
     send, raw1, raw2, alpha0, nq = call(
@@ -432,13 +449,14 @@
     recv = lax.all_to_all(send, "ray", 0, 0)
     send, v1_raw, beta1 = call(
         kernel_next_v,
-        [message, cells, scalar],
+        [((RAY, MSG, LANES), F32), cells, scalar],
         (pos, recv, q_hot, v0_raw, alpha0, nq),
         scratch=[edges],
     )
     recv = lax.all_to_all(send, "ray", 0, 0)
     (send,) = call(
-        kernel_forward, [tile_message], (pos, recv, p_wide, r_hot, first, second, v1_raw), scratch=[(16, LANES)]
+        functools.partial(kernel_forward, last=True), [((TILE, TMSG + 16, LANES), BF16)],
+        (pos, recv, p_wide, r_hot, first, second, v1_raw), scratch=[(16, LANES)],
     )
     recv = lax.all_to_all(send, "tile", 0, 0)
     send, raw1_own, alpha1 = call(

time: 121 us -> 123 us (1.017)
  blocking collectives: 89.5 us -> 91.5 us
where the time goes in v5:
time: 123 us; the launch traced here: 122 us
  blocking collectives  91.5 us (74%)
  Pallas kernels  13.1 us (11%)
  starting transfers between devices  9.01 us (7%)
  waiting for transfers between devices  4.49 us (4%)
  local copies, waits for them, and re-layouts  1.97 us (2%)
  between operations  1.36 us (1%)
    all_to_all x5, blocking collectives, shards(): recv = lax.all_to_all(send, 'ray', 0, 0)  62.8 us
    all_to_all x2, blocking collectives, shards(): recv = lax.all_to_all(send, 'tile', 0, 0)  28.7 us
    pallas_call x9, Pallas kernels, call(): pl.pallas_call(kernel, out_shape=[jax.ShapeDtypeStruct(shape, kind) for s...  13.1 us
    all_to_all x1, starting transfers between devices, shards(): lax.all_to_all(jnp.broadcast_to(own, (TILE,) + own.shape), 'tile', 0, 0)  9.01 us
    all_to_all x1, waiting for transfers between devices, shards(): lax.all_to_all(jnp.broadcast_to(own, (TILE,) + own.shape), 'tile', 0, 0)  4.49 us
  transfers between devices with their start and end apart: 1, of which 1 were waited for; matrix products, arithmetic and copies ran while one was open for 0% of the time, Pallas kernels for 1%

profile of v5, /device:TPU:1, one launch (start us, length us, event | category | flops | bytes accessed | tf_op | source)
XLA Modules:
  0.0 122.2 jit_solution(6520645122756029066)
XLA Ops:
  0.6 0.7 pad_maximum_fusion
  1.4 0.7 broadcast_in_dim.3
  2.0 9.0 %all-to-all-start = ((f32[8,40,128]{2,1,0:T(8,128)}), f32[8,40,128]{2,1,0:T(8,128)S(1)}, u32[]{:S(2)}, u32[]{:S(2)}) async-start(f32[8,40,128]{2,1,0:T(8,128)} %broadcast_in_dim.3), calls=%async_computation | async-start | bytes 327680 | tf_op jit(solution)/shard_map/all_to_all | solution.py:405
  11.7 0.0 copy-start
  11.7 0.6 copy-done
  12.3 0.0 copy-start.1
  12.3 0.7 copy-done.1
  13.0 1.6 %kernel_index.1 = (bf16[256,128]{1,0:T(8,128)(2,1)S(1)}, bf16[128,512]{1,0:T(8,128)(2,1)S(1)}, bf16[64,128]{1,0:T(8,128)(2,1)S(1)}, bf16[128,64]{1,0:T(8,128)(2,...) custom-call(s32[1,128]{1,0:T(1,128)S(1)} %bitcast.9, s32[1,128]{1,0:T(1,128)S(1)} %bitcast.10, ...), custom_call_target="tpu_custom_call" | custom-call | tf_op jit(solution)/shard_map/kernel_index/pallas_call | solution.py:382
  14.6 0.1 pad_add_fusion.pos_ref
  14.7 4.5 %all-to-all-done.start = f32[8,40,128]{2,1,0:T(8,128)S(1)} async-done(((f32[8,40,128]{2,1,0:T(8,128)}), f32[8,40,128]{2,1,0:T(8,128)S(1)}, u32[]{:S(2)}, u32[]{:S(2)}) %all-to-all-start) | async-done | bytes 163872 | tf_op jit(solution)/shard_map/all_to_all | solution.py:405
  19.2 2.5 %kernel_start.1 = (bf16[32,16,128]{2,1,0:T(8,128)(2,1)S(1)}, bf16[64,128,128]{2,1,0:T(8,128)(2,1)S(1)}) custom-call(s32[2]{0:T(128)S(1)} %pad_add_fusion.pos_ref, f32[8,40,128]{2,1,0:T(8,128)S(1)} %all-to-all-done.start, f32[256,128]{1,0:T(8,128)S(1)} %get-tuple-element.27.note, bf16[128,128,128]{2,1,0:T(8,128)(2,1)} %bitcast.12, ...), custom_call_target="tpu_custom_call" | custom-call | tf_op jit(solution)/shard_map/kernel_start/pallas_call | solution.py:382
  21.7 17.2 %all_to_all.40.recv = bf16[32,16,128]{2,1,0:T(8,128)(2,1)S(1)} all-to-all(bf16[32,16,128]{2,1,0:T(8,128)(2,1)S(1)} %get-tuple-element.31), channel_id=1, replica_groups=mesh['ray'=32,'tile'=8] {'ray'}, dimensions={0} | all-to-all | bytes 262144 | tf_op jit(solution)/shard_map/all_to_all | solution.py:430
  38.9 0.9 kernel_first_v.1
  39.8 11.3 %all_to_all.41.recv = bf16[32,16,128]{2,1,0:T(8,128)(2,1)S(1)} all-to-all(bf16[32,16,128]{2,1,0:T(8,128)(2,1)S(1)} %get-tuple-element.32), channel_id=1, replica_groups=mesh['ray'=32,'tile'=8] {'ray'}, dimensions={0} | all-to-all | bytes 262144 | tf_op jit(solution)/shard_map/all_to_all | solution.py:437
  51.1 2.1 %kernel_forward.2 = bf16[8,112,128]{2,1,0:T(8,128)(2,1)S(1)} custom-call(s32[2]{0:T(128)S(1)} %pad_add_fusion.pos_ref, bf16[32,16,128]{2,1,0:T(8,128)(2,1)S(1)} %all_to_all.41.recv, bf16[128,512]{1,0:T(8,128)(2,1)S(1)} %get-tuple-element.33.p_wide, bf16[64,128]{1,0:T(8,128)(2,1)S(1)} %get-tuple-element.34.r_hot, ...), custom_call_target="tpu_custom_call" | custom-call | tf_op jit(solution)/shard_map/kernel_forward/pallas_call | solution.py:382
  53.1 13.9 %all_to_all.42.recv = bf16[8,112,128]{2,1,0:T(8,128)(2,1)S(1)} all-to-all(bf16[8,112,128]{2,1,0:T(8,128)(2,1)S(1)} %kernel_forward.2), channel_id=1, replica_groups=mesh['ray'=32,'tile'=8] {'tile'}, dimensions={0} | all-to-all | bytes 458752 | tf_op jit(solution)/shard_map/all_to_all | solution.py:442
  67.1 1.5 %kernel_back.1 = (bf16[32,16,128]{2,1,0:T(8,128)(2,1)S(1)}, f32[64,128]{1,0:T(8,128)S(1)}, f32[32,8,128]{2,1,0:T(8,128)S(1)}, f32[1,128]{1,0:T(1,128)S(1)}, f32[32,128]{1,0:T(8,128)S(1)}) custom-call(s32[2]{0:T(128)S(1)} %pad_add_fusion.pos_ref, bf16[8,112,128]{2,1,0:T(8,128)(2,1)S(1)} %all_to_all.42.recv, f32[32,128]{1,0:T(8,128)S(1)} %get-tuple-element.36.v_raw.v0_raw, ...), custom_call_target="tpu_custom_call" | custom-call | tf_op jit(solution)/shard_map/kernel_back/pallas_call | solution.py:382
  68.6 11.3 %all_to_all.43.recv = bf16[32,16,128]{2,1,0:T(8,128)(2,1)S(1)} all-to-all(bf16[32,16,128]{2,1,0:T(8,128)(2,1)S(1)} %get-tuple-element.38), channel_id=1, replica_groups=mesh['ray'=32,'tile'=8] {'ray'}, dimensions={0} | all-to-all | bytes 262144 | tf_op jit(solution)/shard_map/all_to_all | solution.py:449
  79.9 0.9 kernel_next_v.1
  80.8 12.6 %all_to_all.44.recv = f32[32,16,128]{2,1,0:T(8,128)S(1)} all-to-all(f32[32,16,128]{2,1,0:T(8,128)S(1)} %get-tuple-element.42), channel_id=1, replica_groups=mesh['ray'=32,'tile'=8] {'ray'}, dimensions={0} | all-to-all | bytes 524288 | tf_op jit(solution)/shard_map/all_to_all | solution.py:456
  93.4 2.1 %kernel_forward.3 = bf16[8,128,128]{2,1,0:T(8,128)(2,1)S(1)} custom-call(s32[2]{0:T(128)S(1)} %pad_add_fusion.pos_ref, f32[32,16,128]{2,1,0:T(8,128)S(1)} %all_to_all.44.recv, bf16[128,512]{1,0:T(8,128)(2,1)S(1)} %get-tuple-element.33.p_wide, bf16[64,128]{1,0:T(8,128)(2,1)S(1)} %get-tuple-element.34.r_hot, ...), custom_call_target="tpu_custom_call" | custom-call | tf_op jit(solution)/shard_map/kernel_forward/pallas_call | solution.py:382
  95.5 14.8 %all_to_all.45.recv = bf16[8,128,128]{2,1,0:T(8,128)(2,1)S(1)} all-to-all(bf16[8,128,128]{2,1,0:T(8,128)(2,1)S(1)} %kernel_forward.3), channel_id=1, replica_groups=mesh['ray'=32,'tile'=8] {'tile'}, dimensions={0} | all-to-all | bytes 524288 | tf_op jit(solution)/shard_map/all_to_all | solution.py:461
  110.3 0.8 kernel_last_norm.1
  111.1 10.5 %all_to_all.46.recv = f32[32,1,128]{2,1,0:T(1,128)S(1)} all-to-all(f32[32,1,128]{2,1,0:T(1,128)S(1)} %get-tuple-element.47), channel_id=1, replica_groups=mesh['ray'=32,'tile'=8] {'ray'}, dimensions={0} | all-to-all | bytes 32768 | tf_op jit(solution)/shard_map/all_to_all | solution.py:468
  121.6 0.7 kernel_end.1
Async XLA Ops:
  2.0 17.2 %all-to-all-start = ((f32[8,40,128]{2,1,0:T(8,128)}), f32[8,40,128]{2,1,0:T(8,128)S(1)}, u32[]{:S(2)}, u32[]{:S(2)}) async-start(f32[8,40,128]{2,1,0:T(8,128)} %broadcast_in_dim.3), calls=%async_computation | async-start | bytes 327680 | tf_op jit(solution)/shard_map/all_to_all | solution.py:405
  11.7 0.7 copy-start
  12.3 0.7 copy-start.1
